TPU v7x, 128 devices: a whole 4x4x4 slice. The times are simulated.
128 devices in a mesh: section: 2 (over z_hi), dp: 64 (over z_lo, x, y, core).
Axes of the slice: x: 4, y: 4, z: 4 (z_hi: 2, z_lo: 2; z = z_hi * 2 + z_lo), core: 2. Of those that a mesh axis runs over, the one named last changes fastest.
Arguments:
- fields: bfloat16 [16384, 640], P('dp'), may hold values from -6 to 6
- behaviour: bfloat16 [16384, 3200], P('dp'), may hold values from -6 to 6
- lengths: int32 [16384], P('dp'), may hold values from 1 to 200, as said below
- domains: int32 [16384], P('dp'), may hold values from 0 to 1
- validity: int32 [16384], P('dp'), may hold values from 0 to 1, as said below
- cotangent: float32 [16384], P('dp'), may hold values from -6 to 6
- w_query: float32 [16, 16], replicated, may hold values from -1.5 to 1.5
- w_key: float32 [16, 16], replicated, may hold values from -1.5 to 1.5
- w_value: float32 [16, 16], replicated, may hold values from -1.5 to 1.5
- w_proj: bfloat16 [640, 512], replicated, may hold values from -0.25 to 0.25
- b_proj: float32 [512], replicated, may hold values from -0.6 to 0.6
- norm_gain: float32 [512], replicated, may hold values from 0.5 to 1.5
- norm_shift: float32 [512], replicated, may hold values from -0.6 to 0.6
- gate_weight: bfloat16 [512, 7], replicated, may hold values from -0.1875 to 0.1875
- w_in: bfloat16 [6, 512, 1024], replicated, may hold values from -0.25 to 0.25
- b_in: float32 [6, 1024], replicated, may hold values from -0.6 to 0.6
- w_out: bfloat16 [6, 1024, 512], replicated, may hold values from -0.1875 to 0.1875
- b_out: float32 [6, 512], replicated, may hold values from -0.6 to 0.6
- tower_in: bfloat16 [512, 512], replicated, may hold values from -0.25 to 0.25
- tower_bias: float32 [512], replicated, may hold values from -0.6 to 0.6
- tower_out: float32 [512], replicated, may hold values from -0.375 to 0.375
- tower_end: float32 [2], replicated, may hold values from -3 to 3
Outputs:
- predictions: float32 [2, 16384], P('section', 'dp')
- field_grad: float32 [2, 16384, 640], P('section', 'dp')
- behaviour_grad: float32 [2, 16384, 3200], P('section', 'dp')
- query_grad: float32 [2, 16, 16], P('section')
- key_grad: float32 [2, 16, 16], P('section')
- value_grad: float32 [2, 16, 16], P('section')
- proj_grad: float32 [2, 640, 512], P('section')
- proj_bias_grad: float32 [2, 512], P('section')
- gain_grad: float32 [2, 512], P('section')
- shift_grad: float32 [2, 512], P('section')
- gate_grad: float32 [2, 512, 7], P('section')
- in_grad: float32 [2, 6, 512, 1024], P('section')
- in_bias_grad: float32 [2, 6, 1024], P('section')
- out_grad: float32 [2, 6, 1024, 512], P('section')
- out_bias_grad: float32 [2, 6, 512], P('section')
- tower_in_grad: float32 [2, 512, 512], P('section')
- tower_bias_grad: float32 [2, 512], P('section')
- tower_out_grad: float32 [2, 512], P('section')
- tower_end_grad: float32 [2, 2], P('section')
- root_means: float32 [2, 2], P('section')
Inputs may be any that keep to these rules, and one draw needn't show every extreme that they name: `lengths`: the first event of every aligned block of 64 events has length 200. `validity`: the first event of every aligned block of 64 events is valid.
All inputs are finite; a program needn't handle non-finite values.
Results may differ from a plain program's by a relative error of at most 0.011.
Values may be sent and summed in bfloat16 or wider, within the bound.
A program may use at most 256 MiB of HBM per device.

v0:
```python
import jax
import jax.numpy as jnp
from jax import lax
from jax.experimental import pallas as pl
from jax.experimental.pallas import tpu as pltpu
from jax.sharding import PartitionSpec as P

EPSILON = 1e-05
MESH = pl.DeviceIdType.MESH
F32 = jnp.float32
BF16 = jnp.bfloat16

LANES = 128
DIMS = 5
HALVINGS = 3
SLOTS = 7 + HALVINGS
ROWS = 256
EXPERTS = 6
HIDDEN = 512
WIDE = 1024
FIELDS = 640
EMBED = 16
SEQ = 3200
SPAN = 256
PIECES = tuple((at, SPAN) for at in range(0, 3072, SPAN)) + ((3072, LANES),)
PROJ_ROWS = 256
SMALL_ROWS = 128
BLOCK = 64


def coords():
    section, place = lax.axis_index("section"), lax.axis_index("dp")
    return 2 * section + place // 32, (place // 8) % 4, (place // 2) % 4, place % 2


def device_at(z, x, y, core):
    return {"section": z // 2, "dp": (((z % 2) * 4 + x) * 4 + y) * 2 + core}


def hop(r, kind):
    near, far = 1 - 2 * (r % 2), 3 - 2 * r
    return near + kind * (far - near)


def side(r, kind):
    near = (r + r // 2) % 2
    return near + kind * (r // 2 - near)


def picks(dim):
    a = dim % 3
    return (1 - a) * (2 - a) // 2, a * (2 - a), a * (a - 1) // 2, dim // 3


def neighbour(dim):
    z, x, y, core = coords()
    ex, ey, ez, kind = picks(dim)
    return device_at(z + ez * hop(z, kind), x + ex * hop(x, kind), y + ey * hop(y, kind), core)


def which_half(dim):
    z, x, y, core = coords()
    ex, ey, ez, kind = picks(dim)
    return ex * side(x, kind) + ey * side(y, kind) + ez * side(z, kind)


def sibling():
    z, x, y, core = coords()
    return device_at(z, x, y, 1 - core)


def cross():
    z, x, y, core = coords()
    return device_at(3 - z, x, y, core)


class Family:
    def __init__(self, rows, out, refs, first, to_other=False):
        self.rows = rows
        self.share = rows >> HALVINGS
        self.out = out
        self.first = first
        self.to_other = to_other
        (
            self.kept,
            self.arrived,
            self.doubled,
            self.pair_send,
            self.pair_recv,
            self.send_sem,
            self.recv_sem,
        ) = refs

    def total(self, units, rows=slice(None)):
        return self.out.at[units, coords()[3], rows]

    def remote(self, unit, slot, src, dst, to):
        return pltpu.make_async_remote_copy(
            src_ref=src,
            dst_ref=dst,
            send_sem=self.send_sem.at[slot],
            recv_sem=self.recv_sem.at[unit // DIMS, slot],
            device_id=to,
            device_id_type=MESH,
        )

    def start_of(self, part, step):
        start = 0
        for k in range(step):
            start = start + which_half((part + k) % DIMS) * (self.rows >> (k + 1))
        return start

    def span(self, start, size):
        return pl.ds(pl.multiple_of(start, size), size)

    def own_share(self, unit):
        return self.span(self.start_of(unit % DIMS, HALVINGS), self.share)

    def across(self, group, unit, count):
        return pltpu.make_async_remote_copy(
            src_ref=self.total(pl.ds(unit, count)),
            dst_ref=self.kept.at[pl.ds(unit - self.first, count)],
            send_sem=self.pair_send.at[group],
            recv_sem=self.pair_recv.at[group],
            device_id=sibling(),
            device_id_type=MESH,
        )

    def halve(self, unit, k):
        size = self.rows >> (k + 1)
        dim = (unit + k) % DIMS
        start = self.start_of(unit % DIMS, k) + (1 - which_half(dim)) * size
        local = unit - self.first
        return self.remote(
            unit,
            k,
            self.kept.at[local, self.span(start, size)],
            self.arrived.at[local, pl.ds(self.rows - 2 * size, size)],
            neighbour(dim),
        )

    def double(self, unit, j):
        local = unit - self.first
        src = self.kept.at[local, self.own_share(unit)] if j == 0 else self.doubled.at[local, j - 1]
        return self.remote(
            unit,
            HALVINGS + j,
            src,
            self.arrived.at[local, pl.ds(self.rows - self.share + j * self.share, self.share)],
            neighbour((unit + HALVINGS + j) % DIMS),
        )

    def over(self, unit):
        region = self.total(unit, self.own_share(unit))
        return self.remote(unit, DIMS, region, region, cross())

    def spread(self, unit, k):
        size = self.rows >> (k + 1)
        region = self.total(unit, self.span(self.start_of(unit % DIMS, k + 1), size))
        return self.remote(unit, DIMS + 1 + k, region, region, neighbour((unit + k) % DIMS))

    def back(self, unit):
        return self.remote(unit, DIMS + 1 + HALVINGS, self.total(unit), self.total(unit), sibling())

    def send(self, group, unit, halves):
        for i, rows in enumerate(halves):
            self.out[unit + i, coords()[3]] = rows.astype(self.out.dtype)
        self.across(group, unit, len(halves)).start()

    def take(self, group, unit, halves):
        pair = self.across(group, unit, len(halves))
        pair.wait_send()
        pair.wait_recv()
        for i, rows in enumerate(halves):
            local = unit + i - self.first
            self.kept[local] = (rows + self.kept[local].astype(F32)).astype(self.kept.dtype)
            self.halve(unit + i, 0).start()

    def await_chunk(self, slot, base, ref):
        pltpu.make_async_copy(ref, ref, self.recv_sem.at[base // DIMS, slot]).wait()

    def each(self, base, count, work):
        def one(i, _):
            work(base + i)
            return 0

        lax.fori_loop(0, count, one, 0)

    def reduce(self, base, count, step):
        dtype = self.kept.dtype
        local = pl.ds(base - self.first, count)
        if step < HALVINGS:
            size = self.rows >> (step + 1)
            arrivals = pl.ds(self.rows - 2 * size, size)
        else:
            size = self.share
            arrivals = pl.ds(self.rows - size + (step - HALVINGS) * size, size)
        self.await_chunk(step, base, self.arrived.at[local, arrivals])

        def one(unit):
            here = unit - self.first
            came = self.arrived[here, arrivals].astype(F32)
            if step < HALVINGS:
                region = self.span(self.start_of(unit % DIMS, step + 1), size)
                self.kept[here, region] = (self.kept[here, region].astype(F32) + came).astype(dtype)
                if step + 1 < HALVINGS:
                    self.halve(unit, step + 1).start()
                else:
                    self.double(unit, 0).start()
                return
            j = step - HALVINGS
            region = self.own_share(unit)
            old = self.kept[here, region] if j == 0 else self.doubled[here, j - 1]
            new = (old.astype(F32) + came).astype(dtype)
            if step + 1 < DIMS:
                self.doubled[here, j] = new
                self.double(unit, j + 1).start()
            else:
                self.out[unit, coords()[3], region] = new
                if self.to_other:
                    self.over(unit).start()
                else:
                    self.spread(unit, HALVINGS - 1).start()

        self.each(base, count, one)

    def gather(self, base, count, step):
        units = pl.ds(base, count)
        if step == 0:
            self.await_chunk(DIMS, base, self.total(units, pl.ds(0, self.share)))
            self.each(base, count, lambda unit: self.spread(unit, HALVINGS - 1).start())
        elif step <= HALVINGS:
            k = HALVINGS - step
            self.await_chunk(DIMS + 1 + k, base, self.total(units, pl.ds(0, self.rows >> (k + 1))))

            def one(unit):
                if k > 0:
                    self.spread(unit, k - 1).start()
                else:
                    self.back(unit).start()

            self.each(base, count, one)
        else:
            self.await_chunk(DIMS + 1 + HALVINGS, base, self.out.at[units, 1 - coords()[3]])

    def drain(self, reduced, gathered):
        def sent(slot, ref):
            pltpu.make_async_copy(ref, ref, self.send_sem.at[slot]).wait()

        for step in range(DIMS):
            size = self.rows >> (step + 1) if step < HALVINGS else self.share
            sent(step, self.kept.at[pl.ds(0, reduced), pl.ds(0, size)])
        if self.to_other:
            sent(DIMS, self.kept.at[pl.ds(0, reduced), pl.ds(0, self.share)])
        if gathered:
            for k in range(HALVINGS):
                sent(DIMS + 1 + k, self.total(pl.ds(0, gathered), pl.ds(0, self.rows >> (k + 1))))
            sent(DIMS + 1 + HALVINGS, self.total(pl.ds(0, gathered)))


def family_scratch(units, reduced, groups, rows, dtype):
    share = rows >> HALVINGS
    chunks = pl.cdiv(units, DIMS)
    return [
        pltpu.VMEM((reduced, rows, LANES), dtype),
        pltpu.VMEM((reduced, rows - share + (DIMS - HALVINGS) * share, LANES), dtype),
        pltpu.VMEM((reduced, max(1, DIMS - HALVINGS - 1), share, LANES), dtype),
        pltpu.SemaphoreType.DMA((groups,)),
        pltpu.SemaphoreType.DMA((groups,)),
        pltpu.SemaphoreType.DMA((SLOTS,)),
        pltpu.SemaphoreType.DMA((chunks, SLOTS)),
    ]


FAMILIES = ((25, 15, 13, 1024, BF16), (DIMS, DIMS, 1, PROJ_ROWS, BF16), (1, 1, 1, SMALL_ROWS, F32))
TOWER_UNIT = 12
IN_UNIT = 13
SPLIT = 15
TINY_ROWS = 24


PLAN_FIRST = (
    ("ins", 1, 6), ("back", 0, 1), ("sum", 3, 0), ("front",), ("sum", 3, 1), ("sum", 4, 0), ("send_p",), ("sum", 3, 2),
    ("sum", 4, 1), ("take_p",), ("sum", 3, 3), ("sum", 4, 2), ("sum", 3, 4), ("sum", 4, 3), ("sum_p", 0), ("sum", 4, 4),
    ("sum_p", 1), ("seq", 0, 2), ("sum_p", 2), ("seq", 2, 4), ("sum_p", 3), ("weights",), ("tiny", 0), ("sum_p", 4),
    ("tiny", 1), ("all_p", 1), ("tiny", 2), ("all_p", 2), ("tiny", 3), ("all_p", 3), ("tiny", 4), ("all_p", 4),
    ("tiny", 5), ("tiny", 6),
)
PLAN_SECOND = (
    ("outs", 0, 6), ("tower",), ("ins", 0, 1), ("sum", 0, 0), ("back", 1, 3), ("sum", 1, 0), ("sum", 0, 1),
    ("back", 3, 6), ("sum", 0, 2), ("sum", 1, 1), ("sum", 2, 0), ("front",), ("sum", 0, 3), ("sum", 1, 2), ("sum", 2, 1),
    ("send_v",), ("sum", 0, 4), ("sum", 1, 3), ("sum", 2, 2), ("take_v",), ("all", 0, 1), ("sum", 1, 4), ("sum", 2, 3),
    ("sum_v", 0), ("all", 0, 2), ("all", 1, 1), ("sum", 2, 4), ("sum_v", 1), ("all", 3, 0), ("all", 0, 3), ("all", 1, 2),
    ("all", 2, 1), ("sum_v", 2), ("all", 3, 1), ("all", 4, 0), ("all", 1, 3), ("all", 2, 2), ("sum_v", 3), ("all", 0, 4),
    ("all", 3, 2), ("all", 4, 1), ("sum_v", 4), ("all", 2, 3), ("all", 1, 4), ("all_v", 1), ("all", 3, 3), ("all", 4, 2),
    ("all_v", 2), ("all", 2, 4), ("all", 4, 3), ("all_v", 3), ("all", 3, 4), ("all_v", 4), ("all", 4, 4),
)


def exact(left, right):
    return jnp.dot(left, right, precision=lax.Precision.HIGHEST, preferred_element_type=F32)


def exact_cols(left, right):
    return lax.dot_general(
        left, right, (((1,), (1,)), ((), ())), precision=lax.Precision.HIGHEST, preferred_element_type=F32
    )


def exact_rows(left, right):
    return lax.dot_general(
        left, right, (((0,), (0,)), ((), ())), precision=lax.Precision.HIGHEST, preferred_element_type=F32
    )


def product(left, right):
    return jnp.dot(left, right, preferred_element_type=F32)


def contract_rows(left, right):
    return lax.dot_general(left, right, (((0,), (0,)), ((), ())), preferred_element_type=F32)


def contract_cols(left, right):
    return lax.dot_general(left, right, (((1,), (1,)), ((), ())), preferred_element_type=F32)


def split(value, terms):
    out = []
    for _ in range(terms):
        out.append(value.astype(BF16))
        value = value - out[-1].astype(F32)
    return out


def sigmoid(v):
    return 1.0 / (1.0 + jnp.exp(-v))


ROOT = 0.7978845608028654
CUBE = 0.044715


def gelu_both(v):
    square = v * v
    bent = jnp.tanh(v * (ROOT + ROOT * CUBE * square))
    half = 0.5 + 0.5 * bent
    slope = half + 0.5 * v * (1.0 - bent * bent) * (ROOT + 3.0 * ROOT * CUBE * square)
    return v * half, slope


def column_sum(array):
    return jnp.sum(array, axis=0, keepdims=True)


def row_sum(array):
    return jnp.sum(array, axis=1, keepdims=True)


def lanes(shape):
    return lax.broadcasted_iota(jnp.int32, shape, 1)


def lane_match(rows, columns, period, shift=0):
    place = lax.broadcasted_iota(jnp.int32, (rows, columns), 1) - shift
    if period:
        place = place % period
    return (place == lax.broadcasted_iota(jnp.int32, (rows, columns), 0)).astype(F32)


def kernel(
    fields,
    lengths,
    domains,
    validity,
    cotangent,
    w_query,
    w_key,
    w_value,
    w_proj,
    b_proj,
    norm_gain,
    norm_shift,
    gate_turned,
    b_in,
    b_out,
    tower_in,
    tower_bias,
    tower_out,
    tower_end,
    behaviour_hbm,
    w_in_hbm,
    w_out_hbm,
    big_out,
    proj_out,
    small_out,
    tiny_out,
    pred_all,
    d_fields,
    d_seq,
    behaviour,
    w_in,
    w_out,
    groups,
    probe_w,
    value_w,
    pooled_w,
    back_w,
    target_w,
    proj_turned,
    gate_rows,
    info,
    joined,
    activation,
    proj_slope,
    normed,
    standard,
    active,
    slope,
    expert,
    d_expert,
    d_normed,
    d_residual,
    mixing,
    d_mixing,
    gates,
    residual_low,
    d_tower,
    d_proj_low,
    pooled_rows,
    d_value_rows,
    d_probe_rows,
    small,
    tiny,
    tiny_arrived,
    load_sem,
    tiny_send,
    tiny_recv,
    *family_refs,
):
    section = lax.axis_index("section")
    core = coords()[3]

    barrier = pltpu.get_barrier_semaphore()
    for dim in range(DIMS):
        pl.semaphore_signal(barrier, inc=1, device_id=neighbour(dim), device_id_type=MESH)
    for other in (sibling(), cross()):
        pl.semaphore_signal(barrier, inc=1, device_id=other, device_id_type=MESH)

    seq_copy = pltpu.make_async_copy(behaviour_hbm, behaviour, load_sem.at[12])

    def load_in(e):
        return pltpu.make_async_copy(w_in_hbm.at[e], w_in.at[e], load_sem.at[e])

    def load_out(e):
        return pltpu.make_async_copy(w_out_hbm.at[e], w_out.at[e], load_sem.at[6 + e])

    tile = lane_match(EMBED, SPAN, EMBED)

    def prepare():
        seq_copy.start()
        for e in range(EXPERTS):
            load_in(e).start()
            load_out(e).start()
        group = lax.broadcasted_iota(jnp.int32, (SPAN, SPAN), 0) // EMBED
        groups[...] = (group == lanes((SPAN, SPAN)) // EMBED).astype(F32).astype(BF16)
        eye = lane_match(EMBED, LANES, 0)
        probe_w[...] = exact(w_query[...], exact_rows(w_key[...], tile))
        value_w[...] = exact_rows(tile, exact(w_value[...], eye))
        pooled_w[...] = exact_rows(tile, eye)
        back_w[...] = exact_rows(w_value[...], tile)
        target_w[...] = exact_rows(tile, exact(exact_cols(w_key[...], w_query[...]), eye))
        proj_turned[:EMBED] = w_proj[FIELDS - EMBED :]
        proj_turned[EMBED:] = w_proj[: FIELDS - EMBED]
        rows = [lengths[...].astype(F32), domains[...].astype(F32), validity[...].astype(F32), cotangent[...]]
        info[...] = jnp.transpose(jnp.concatenate(rows + [jnp.zeros((4, ROWS), F32)], axis=0))
        gate_rows[...] = jnp.zeros_like(gate_rows)
        gate_rows[:7] = gate_turned[...]
        small[...] = jnp.zeros_like(small)
        tiny[0] = jnp.zeros((TINY_ROWS, LANES), F32)
        seq_copy.wait()

    def group_sum(value, terms):
        count, width = value.shape
        stacked = jnp.concatenate(split(value, terms), axis=0)
        sums = product(stacked, groups[:width, :width])
        return sum(sums[i * count : (i + 1) * count] for i in range(terms))

    def narrow_sum(pieces):
        wide = sum(pieces[:-1])
        return jnp.concatenate([wide[:, :LANES] + pieces[-1], wide[:, LANES:]], axis=1)

    def stretch(rows, at, width):
        return behaviour[rows, at : at + width].astype(F32)

    def attention(rows):
        target = fields[rows, 0:LANES].astype(F32)[:, :EMBED]
        probe = exact(target, probe_w[...])
        length = info[rows, 0:1]
        scores = []
        for at, width in PIECES:
            sums = group_sum(stretch(rows, at, width) * probe[:, :width], 3)
            place = ((lanes((1, width)) + at) // EMBED).astype(F32)
            scores.append(jnp.where(place < length, 0.5 * sums, -1e30))
        peak = scores[0]
        for piece in scores[1:-1]:
            peak = jnp.maximum(peak, piece)
        peak = jnp.maximum(jnp.max(peak, axis=1, keepdims=True), jnp.max(scores[-1], axis=1, keepdims=True))
        raised = [jnp.exp(piece - peak) for piece in scores]
        scale = float(EMBED) / row_sum(narrow_sum(raised))
        return probe, [piece * scale for piece in raised]

    def pool(rows, attn):
        return narrow_sum([w * stretch(rows, at, width) for w, (at, width) in zip(attn, PIECES)])

    def attention_forward(block, _):
        rows = pl.ds(pl.multiple_of(block * BLOCK, BLOCK), BLOCK)
        _, attn = attention(rows)
        value = exact(pool(rows, attn), value_w[...])
        joined[rows, LANES:] = fields[rows, LANES:]
        head = fields[rows, :LANES]
        joined[rows, :LANES] = jnp.where(lanes(head.shape) < EMBED, value.astype(BF16), head)
        return 0

    def gate_columns():
        return [gates[:, i : i + 1] for i in range(6)]

    def front_forward():
        projected = product(joined[...], proj_turned[...]) + b_proj[...]
        act, slope_proj = gelu_both(projected)
        act = act.astype(BF16).astype(F32)
        activation[...] = act
        proj_slope[...] = slope_proj
        centred = act - row_sum(act) * (1.0 / HIDDEN)
        scale = lax.rsqrt(row_sum(centred * centred) * (1.0 / HIDDEN) + EPSILON)
        standard[...] = centred * scale
        normed[...] = (centred * scale * norm_gain[...] + norm_shift[...]).astype(BF16)

        logits = contract_cols(normed[...], gate_rows[...])
        in_first = info[:, 1:2] == 0.0
        level = sigmoid(logits[:, 6:7])
        shared_a = sigmoid(logits[:, 0:1] - logits[:, 1:2])
        shared_b = sigmoid(logits[:, 1:2] - logits[:, 0:1])
        lead = jnp.where(in_first, logits[:, 2:3] - logits[:, 3:4], logits[:, 4:5] - logits[:, 5:6])
        chosen_a, chosen_b = sigmoid(lead), sigmoid(-lead)
        zero = jnp.zeros_like(level)
        columns = [
            level * shared_a,
            level * shared_b,
            jnp.where(in_first, (1.0 - level) * chosen_a, zero),
            jnp.where(in_first, (1.0 - level) * chosen_b, zero),
            jnp.where(in_first, zero, (1.0 - level) * chosen_a),
            jnp.where(in_first, zero, (1.0 - level) * chosen_b),
        ]
        place = lanes((ROWS, 8))
        mixing[...] = sum(jnp.where(place == i, column, 0.0) for i, column in enumerate(columns))
        held = (scale, level, shared_a, shared_b, chosen_a, chosen_b)
        gates[...] = sum(jnp.where(place == i, column, 0.0) for i, column in enumerate(held))
        d_residual[...] = jnp.zeros_like(d_residual)

    def expert_forward(e, _):
        load_in(e).wait()
        load_out(e).wait()
        pre = product(normed[...], w_in[e]) + b_in[pl.ds(e, 1)]
        out, grade = gelu_both(pre)
        active[e] = out.astype(BF16)
        slope[e] = grade.astype(BF16)
        rows = product(active[e], w_out[e]) + b_out[pl.ds(e, 1)]
        expert[e] = rows.astype(BF16)
        weight = row_sum(jnp.where(lanes((ROWS, 8)) == e, mixing[...], 0.0))
        d_residual[...] += weight * rows
        return 0

    def tower_both():
        branch = d_residual[...]
        residual = activation[...] + branch
        in_first = info[:, 1:2] == 0.0
        valid = info[:, 2:3]
        residual_low[...] = residual.astype(BF16)
        tower_act, tower_slope = gelu_both(product(residual_low[...], tower_in[...]) + tower_bias[...])
        chosen = jnp.where(in_first, 0, 1) == lanes((ROWS, HIDDEN)) // 256
        ends = tower_end[...]
        end = jnp.where(in_first, ends[:, 0:1], ends[:, 1:2])
        predict = sigmoid(row_sum(jnp.where(chosen, tower_act * tower_out[...], 0.0)) + end)
        d_logit = info[:, 3:4] * valid * predict * (1.0 - predict)
        spread_logit = jnp.where(chosen, d_logit, 0.0)
        d_tower[...] = (spread_logit * tower_out[...] * tower_slope).astype(BF16)
        small[3:4] = column_sum(d_tower[...].astype(F32))
        small[4:5] = column_sum(tower_act * spread_logit)
        spots = lanes((1, HIDDEN))
        parts = (
            column_sum(jnp.where(in_first, d_logit, 0.0)),
            column_sum(jnp.where(in_first, 0.0, d_logit)),
            column_sum(valid * row_sum(residual * residual)),
            column_sum(valid * row_sum(branch * branch)),
            column_sum(valid),
        )
        small[5:6] = sum(jnp.where(spots == i, part, 0.0) for i, part in enumerate(parts))
        wide = jnp.transpose(jnp.broadcast_to(predict, (ROWS, LANES)))
        pred_all[0] = wide[:8, :LANES]
        pred_all[1] = wide[:8, LANES:]
        d_residual[...] = contract_cols(d_tower[...], tower_in[...])

    def spread_residual(e, _):
        weight = row_sum(jnp.where(lanes((ROWS, 8)) == e, mixing[...], 0.0))
        low = (weight * d_residual[...]).astype(BF16)
        d_expert[e] = low
        small[pl.ds(32 + e, 1)] = column_sum(low.astype(F32))
        inner = row_sum(expert[e].astype(F32) * d_residual[...])
        d_mixing[...] = jnp.where(lanes((ROWS, 8)) == e, inner, d_mixing[...])
        return 0

    def expert_backward(e, _):
        grade = contract_cols(d_expert[e], w_out[e]) * slope[e].astype(F32)
        low = grade.astype(BF16)
        slope[e] = low
        sums = column_sum(low.astype(F32))
        small[pl.ds(16 + e, 1)] = sums[:, :512]
        small[pl.ds(24 + e, 1)] = sums[:, 512:]
        d_normed[...] += contract_cols(low, w_in[e])
        return 0

    def front_backward():
        scale, level, shared_a, shared_b, chosen_a, chosen_b = gate_columns()
        in_first = info[:, 1:2] == 0.0
        grads = [d_mixing[:, e : e + 1] for e in range(EXPERTS)]
        grad_a = jnp.where(in_first, grads[2], grads[4])
        grad_b = jnp.where(in_first, grads[3], grads[5])
        d_level = grads[0] * shared_a + grads[1] * shared_b - grad_a * chosen_a - grad_b * chosen_b
        d_shared = level * shared_a * shared_b * (grads[0] - grads[1])
        d_lead = (1.0 - level) * chosen_a * chosen_b * (grad_a - grad_b)
        zero = jnp.zeros_like(d_lead)
        d_first = jnp.where(in_first, d_lead, zero)
        d_second = jnp.where(in_first, zero, d_lead)
        columns = (d_shared, -d_shared, d_first, -d_first, d_second, -d_second, d_level * level * (1.0 - level))
        place = lanes((ROWS, LANES))
        d_logits = sum(jnp.where(place == i, column, 0.0) for i, column in enumerate(columns)).astype(BF16)
        small[8:16] = jnp.transpose(contract_rows(normed[...], d_logits))[:8]
        total = d_normed[...] + product(d_logits[:, :16], gate_rows[...])
        std = standard[...]
        small[1:2] = column_sum(total * std)
        small[2:3] = column_sum(total)
        scaled = total * norm_gain[...]
        inner = scaled - row_sum(scaled) * (1.0 / HIDDEN) - std * (row_sum(scaled * std) * (1.0 / HIDDEN))
        d_act = (inner * scale + d_residual[...]).astype(BF16).astype(F32)
        low = (d_act * proj_slope[...]).astype(BF16)
        sums = column_sum(low.astype(F32))
        for i in range(HIDDEN // LANES):
            tiny[0, 16 + i : 17 + i] = sums[:, i * LANES : (i + 1) * LANES]
        d_proj_low[...] = low

    def attention_back(block):
        rows = pl.ds(pl.multiple_of(block * BLOCK, BLOCK), BLOCK)
        probe, attn = attention(rows)
        pooled_rows[rows] = exact(pool(rows, attn), pooled_w[...])
        d_joined = contract_cols(d_proj_low[rows], proj_turned[...])
        head = d_joined[:, :LANES]
        d_value_rows[rows] = head
        d_pooled = exact(head[:, :EMBED], back_w[...])
        d_attn = [group_sum(stretch(rows, at, width) * d_pooled[:, :width], 2) for at, width in PIECES]
        inner = row_sum(narrow_sum([a * d for a, d in zip(attn, d_attn)])) * (1.0 / EMBED)
        pieces = []
        for (at, width), a, d in zip(PIECES, attn, d_attn):
            grade = 0.5 * a * (d - inner)
            pieces.append(grade * stretch(rows, at, width))
            d_seq[rows, at : at + width] = (a * d_pooled[:, :width] + grade * probe[:, :width]).astype(BF16)
        wide = narrow_sum(pieces)
        d_probe_rows[rows] = exact(wide, pooled_w[...])
        d_target = exact(wide, target_w[...])
        d_fields[rows] = d_joined
        d_fields[rows, :LANES] = jnp.where(lanes(head.shape) < EMBED, d_target, head)

    def attention_weights():
        target = fields[:, 0:LANES].astype(F32)[:, :EMBED]
        d_probe = d_probe_rows[...][:, :EMBED]
        query_grad = exact_rows(target, exact(d_probe, w_key[...]))
        key_grad = exact_rows(d_probe, exact(target, w_query[...]))
        value_grad = exact_rows(pooled_rows[...][:, :EMBED], d_value_rows[...][:, :EMBED])
        grads = (query_grad, key_grad, value_grad)
        tiny[0, :EMBED] = sum(exact(g, lane_match(EMBED, LANES, 0, EMBED * i)) for i, g in enumerate(grads))

    def out_halves(e, half):
        grad = contract_rows(active[e], d_expert[e, :, pl.ds(pl.multiple_of(half * 256, 256), 256)])
        return [grad[:, :LANES], grad[:, LANES:]]

    def in_halves(e, half):
        grad = contract_rows(normed[...], slope[e, :, pl.ds(pl.multiple_of(half * 512, 512), 512)])
        columns = [grad[:, i * LANES : (i + 1) * LANES] for i in range(4)]
        return [jnp.concatenate(columns[:2], axis=0), jnp.concatenate(columns[2:], axis=0)]

    def tower_halves(half):
        grad = contract_rows(residual_low[...], d_tower[:, pl.ds(pl.multiple_of(half * 256, 256), 256)])
        return [jnp.concatenate([grad[:, :LANES], grad[:, LANES:]], axis=0)]

    def proj_half(half):
        grad = contract_rows(joined[...], d_proj_low[:, pl.ds(pl.multiple_of(half * 256, 256), 256)])
        columns = []
        for j in range(2):
            column = grad[:, j * LANES : (j + 1) * LANES]
            columns += [column[EMBED:], column[:EMBED]]
        flat = jnp.concatenate(columns, axis=0)
        return [flat[unit * PROJ_ROWS : (unit + 1) * PROJ_ROWS] for unit in range(DIMS)]

    def small_half(half):
        columns = [small[:, pl.ds(pl.multiple_of(half * 256 + j * LANES, LANES), LANES)] for j in range(2)]
        return [jnp.concatenate(columns, axis=0)]

    def tiny_copy(step):
        return pltpu.make_async_remote_copy(
            src_ref=tiny.at[step],
            dst_ref=tiny_arrived.at[step],
            send_sem=tiny_send.at[step],
            recv_sem=tiny_recv.at[step],
            device_id=sibling() if step == DIMS else neighbour(step),
            device_id_type=MESH,
        )

    def tiny_step(step):
        if step:
            tiny_copy(step - 1).wait_recv()
            tiny[step] = tiny[step - 1] + tiny_arrived[step - 1]
        if step <= DIMS:
            tiny_copy(step).start()

    def forward_all():
        prepare()
        lax.fori_loop(0, ROWS // BLOCK, attention_forward, 0)
        front_forward()
        lax.fori_loop(0, EXPERTS, expert_forward, 0)
        tower_both()
        d_normed[...] = jnp.zeros_like(d_normed)
        d_mixing[...] = jnp.zeros_like(d_mixing)
        lax.fori_loop(0, EXPERTS, spread_residual, 0)
        pl.semaphore_wait(barrier, 7)

    def family(i, first=0, to_other=False):
        out = (big_out, proj_out, small_out)[i]
        return Family(FAMILIES[i][3], out, family_refs[7 * i : 7 * i + 7], first, to_other)

    def perform(plan, big, extra):
        def backs(start, end):
            lax.fori_loop(start, end, expert_backward, 0)

        def outs(start, end):
            @pl.loop(start, end + 1)
            def _(e):
                @pl.when(e < end)
                def _():
                    big.send(e, 2 * e, out_halves(e, 1 - core))

                @pl.when(e > start)
                def _():
                    big.take(e - 1, 2 * e - 2, out_halves(e - 1, core))

        def ins(start, end):
            @pl.loop(start, end + 1)
            def _(e):
                @pl.when(e < end)
                def _():
                    expert_backward(e, 0)
                    big.send(6 + e, IN_UNIT + 2 * e, in_halves(e, 1 - core))

                @pl.when(e > start)
                def _():
                    big.take(5 + e, IN_UNIT + 2 * e - 2, in_halves(e - 1, core))

        def tower():
            big.send(12, TOWER_UNIT, tower_halves(1 - core))
            big.take(12, TOWER_UNIT, tower_halves(core))

        work = {
            "outs": outs,
            "ins": ins,
            "tower": tower,
            "back": backs,
            "front": front_backward,
            "sum": lambda c, step: big.reduce(DIMS * c, DIMS, step),
            "all": lambda c, step: big.gather(DIMS * c, DIMS, step),
            **extra,
        }
        for name, *where in plan:
            work[name](*where)

    forward_all()

    @pl.when(section == 0)
    def _():
        big = family(0, SPLIT, True)
        proj = family(1)
        perform(
            PLAN_FIRST,
            big,
            {
                "seq": lambda start, end: pl.loop(start, end)(attention_back),
                "weights": attention_weights,
                "send_p": lambda: proj.send(0, 0, proj_half(1 - core)),
                "take_p": lambda: proj.take(0, 0, proj_half(core)),
                "sum_p": lambda step: proj.reduce(0, DIMS, step),
                "all_p": lambda step: proj.gather(0, DIMS, step),
                "tiny": tiny_step,
            },
        )
        big.drain(FAMILIES[0][0] - SPLIT, 0)
        proj.drain(DIMS, DIMS)
        for step in range(DIMS + 1):
            tiny_copy(step).wait_send()
        tiny_out[...] = tiny[DIMS + 1]

    @pl.when(section == 1)
    def _():
        big = family(0)
        vectors = family(2)
        perform(
            PLAN_SECOND,
            big,
            {
                "send_v": lambda: vectors.send(0, 0, small_half(1 - core)),
                "take_v": lambda: vectors.take(0, 0, small_half(core)),
                "sum_v": lambda step: vectors.reduce(0, 1, step),
                "all_v": lambda step: vectors.gather(0, 1, step),
            },
        )
        big.drain(SPLIT, FAMILIES[0][0])
        vectors.drain(1, 1)


def run(*args):
    here = pl.BlockSpec(memory_space=pltpu.VMEM)
    far = pl.BlockSpec(memory_space=pl.ANY)

    def keep(*shape, dtype=F32):
        return pltpu.VMEM(shape, dtype)

    scratch = [
        keep(ROWS, SEQ, dtype=BF16),
        keep(EXPERTS, HIDDEN, WIDE, dtype=BF16),
        keep(EXPERTS, WIDE, HIDDEN, dtype=BF16),
        keep(SPAN, SPAN, dtype=BF16),
        keep(EMBED, SPAN),
        keep(SPAN, LANES),
        keep(SPAN, LANES),
        keep(EMBED, SPAN),
        keep(SPAN, LANES),
        keep(FIELDS, HIDDEN, dtype=BF16),
        keep(16, HIDDEN, dtype=BF16),
        keep(ROWS, 8),
        keep(ROWS, FIELDS, dtype=BF16),
        keep(ROWS, HIDDEN),
        keep(ROWS, HIDDEN),
        keep(ROWS, HIDDEN, dtype=BF16),
        keep(ROWS, HIDDEN),
        keep(EXPERTS, ROWS, WIDE, dtype=BF16),
        keep(EXPERTS, ROWS, WIDE, dtype=BF16),
        keep(EXPERTS, ROWS, HIDDEN, dtype=BF16),
        keep(EXPERTS, ROWS, HIDDEN, dtype=BF16),
        keep(ROWS, HIDDEN),
        keep(ROWS, HIDDEN),
        keep(ROWS, 8),
        keep(ROWS, 8),
        keep(ROWS, 8),
        keep(ROWS, HIDDEN, dtype=BF16),
        keep(ROWS, HIDDEN, dtype=BF16),
        keep(ROWS, HIDDEN, dtype=BF16),
        keep(ROWS, LANES),
        keep(ROWS, LANES),
        keep(ROWS, LANES),
        keep(64, HIDDEN),
        keep(DIMS + 2, TINY_ROWS, LANES),
        keep(DIMS + 1, TINY_ROWS, LANES),
        pltpu.SemaphoreType.DMA((13,)),
        pltpu.SemaphoreType.DMA((DIMS + 1,)),
        pltpu.SemaphoreType.DMA((DIMS + 1,)),
    ]
    for family in FAMILIES:
        scratch += family_scratch(*family)
    outs = [pltpu.VMEM((units, 2, rows, LANES), dtype) for units, _, _, rows, dtype in FAMILIES]
    outs += [
        pltpu.VMEM((TINY_ROWS, LANES), F32),
        pltpu.VMEM((2, 8, LANES), F32),
        pltpu.VMEM((ROWS, FIELDS), F32),
        pltpu.VMEM((ROWS, SEQ), BF16),
    ]
    return pl.pallas_call(
        kernel,
        out_shape=outs,
        in_specs=[here] * 19 + [far] * 3,
        out_specs=[here] * 7,
        scratch_shapes=scratch,
        compiler_params=pltpu.CompilerParams(
            collective_id=0, has_side_effects=True, vmem_limit_bytes=46 << 20
        ),
        name="rank_and_sum",
    )(*args)


def place_kernel(
    big,
    proj_units,
    small,
    tiny,
    pred_all,
    field_rows,
    seq_rows,
    out_grad,
    in_grad,
    field_grad,
    seq_grad,
    proj,
    tower,
    predictions,
    b_proj,
    gain,
    shift,
    tower_b,
    tower_o,
    tower_e,
    roots,
    gate,
    in_b,
    out_b,
    query,
    key,
    value,
    out_stage,
    in_stage,
    seq_stage,
    field_stage,
    proj_stage,
    tower_stage,
    out_sem,
    in_sem,
    other_sem,
):
    section = lax.axis_index("section")
    second = (section == 1).astype(F32)

    def out_copy(e, slot):
        return pltpu.make_async_copy(out_stage.at[slot], out_grad.at[0, e], out_sem.at[e])

    def in_copy(e, slot):
        return pltpu.make_async_copy(in_stage.at[slot], in_grad.at[0, e], in_sem.at[e])

    stages = ((seq_stage, seq_grad), (field_stage, field_grad), (proj_stage, proj), (tower_stage, tower))
    others = [pltpu.make_async_copy(stage, grad.at[0], other_sem.at[i]) for i, (stage, grad) in enumerate(stages)]

    @pl.when(section == 0)
    def _():
        out_stage[0] = jnp.zeros((WIDE, HIDDEN), F32)
        in_stage[0] = jnp.zeros((HIDDEN, WIDE), F32)
        for e in range(EXPERTS):
            out_copy(e, 0).start()
            in_copy(e, 0).start()
        seq_stage[...] = seq_rows[...].astype(F32)
        others[0].start()
        field_stage[...] = field_rows[...]
        others[1].start()
        for core in range(2):
            flat = jnp.concatenate([proj_units[i, core].astype(F32) for i in range(DIMS)], axis=0)
            for j in range(2):
                at = slice((2 * core + j) * LANES, (2 * core + j + 1) * LANES)
                proj_stage[:, at] = flat[j * FIELDS : (j + 1) * FIELDS]
        others[2].start()
        tower_stage[...] = jnp.zeros_like(tower_stage)
        others[3].start()
        for e in range(EXPERTS):
            out_copy(e, 0).wait()
            in_copy(e, 0).wait()

    @pl.when(section == 1)
    def _():
        @pl.loop(0, EXPERTS)
        def _(e):
            slot = e % 2

            @pl.when(e > 1)
            def _():
                out_copy(e - 2, slot).wait()

            for core in range(2):
                for j in range(2):
                    at = (2 * core + j) * LANES
                    out_stage[slot, :, at : at + LANES] = big[2 * e + j, core].astype(F32)
            out_copy(e, slot).start()

            @pl.when(e > 1)
            def _():
                in_copy(e - 2, slot).wait()

            for core in range(2):
                for j in range(2):
                    for i in range(2):
                        at = (4 * core + 2 * j + i) * LANES
                        rows = slice(i * HIDDEN, (i + 1) * HIDDEN)
                        in_stage[slot, :, at : at + LANES] = big[IN_UNIT + 2 * e + j, core, rows].astype(F32)
            in_copy(e, slot).start()

        for core in range(2):
            for j in range(2):
                at = slice((2 * core + j) * LANES, (2 * core + j + 1) * LANES)
                tower_stage[:, at] = big[TOWER_UNIT, core, j * HIDDEN : (j + 1) * HIDDEN].astype(F32)
        seq_stage[...] = jnp.zeros_like(seq_stage)
        field_stage[...] = jnp.zeros_like(field_stage)
        proj_stage[...] = jnp.zeros_like(proj_stage)
        for other in others:
            other.start()
        for e in (EXPERTS - 2, EXPERTS - 1):
            out_copy(e, e % 2).wait()
            in_copy(e, e % 2).wait()

    for j in range(2):
        predictions[:, j * LANES : (j + 1) * LANES] = jnp.where(section == 1, pred_all[j, 0:1], 0.0)

    def rows(start, count):
        found = jnp.concatenate(
            [small[0, core, j * 64 + start : j * 64 + start + count] for core in range(2) for j in range(2)],
            axis=1,
        )
        return jnp.where(section == 1, found, 0.0)

    head = rows(0, 8)
    gain[...] = head[1:2]
    shift[...] = head[2:3]
    tower_b[...] = head[3:4]
    tower_o[...] = head[4:5]
    tower_e[...] = head[5:6, 0:2]
    count = head[5:6, 4:5]
    squares = head[5:6, 2:4] / (float(HIDDEN) * jnp.maximum(count, 1.0)) + EPSILON
    roots[...] = jnp.where(count > 0.0, jnp.sqrt(squares), 0.0) * second
    gate_lines, out_lines = rows(8, 8), rows(32, 8)
    in_lines = jnp.concatenate([rows(16, 8), rows(24, 8)], axis=1)
    for i in range(7):
        gate[i] = gate_lines[i : i + 1]
    for e in range(EXPERTS):
        in_b[e] = in_lines[e : e + 1]
        out_b[e] = out_lines[e : e + 1]
    three = jnp.where(section == 0, tiny[...], 0.0)
    b_proj[...] = jnp.concatenate([three[16 + i : 17 + i] for i in range(4)], axis=1)
    query[0] = three[:EMBED, 0:16]
    key[0] = three[:EMBED, 16:32]
    value[0] = three[:EMBED, 32:48]
    for other in others:
        other.wait()


def place(*results):
    here = pl.BlockSpec(memory_space=pltpu.VMEM)
    far = pl.BlockSpec(memory_space=pl.ANY)
    shapes = [(1, 6, 1024, 512), (1, 6, 512, 1024), (1, ROWS, FIELDS), (1, ROWS, SEQ), (1, 640, 512), (1, 512, 512)]
    shapes += [(1, ROWS)] + [(1, 512)] * 5 + [(1, 2)] * 2
    shapes += [(7, 1, 512), (6, 1, 1024), (6, 1, 512)] + [(1, 16, 16)] * 3
    return pl.pallas_call(
        place_kernel,
        out_shape=[jax.ShapeDtypeStruct(shape, F32) for shape in shapes],
        in_specs=[here] * 7,
        out_specs=[far] * 6 + [here] * 14,
        scratch_shapes=[
            pltpu.VMEM((2, WIDE, HIDDEN), F32),
            pltpu.VMEM((2, HIDDEN, WIDE), F32),
            pltpu.VMEM((ROWS, SEQ), F32),
            pltpu.VMEM((ROWS, FIELDS), F32),
            pltpu.VMEM((FIELDS, HIDDEN), F32),
            pltpu.VMEM((HIDDEN, HIDDEN), F32),
            pltpu.SemaphoreType.DMA((EXPERTS,)),
            pltpu.SemaphoreType.DMA((EXPERTS,)),
            pltpu.SemaphoreType.DMA((4,)),
        ],
        compiler_params=pltpu.CompilerParams(vmem_limit_bytes=24 << 20),
        name="place",
    )(*(pltpu.with_memory_space_constraint(result, pltpu.VMEM) for result in results))


def body(
    fields,
    behaviour,
    lengths,
    domains,
    validity,
    cotangent,
    w_query,
    w_key,
    w_value,
    w_proj,
    b_proj,
    norm_gain,
    norm_shift,
    gate_weight,
    w_in,
    b_in,
    w_out,
    b_out,
    tower_in,
    tower_bias,
    tower_out,
    tower_end,
):
    def line(array):
        return array.reshape(1, -1)

    results = run(
        fields,
        line(lengths),
        line(domains),
        line(validity),
        line(cotangent),
        w_query,
        w_key,
        w_value,
        w_proj,
        line(b_proj),
        line(norm_gain),
        line(norm_shift),
        gate_weight.T,
        b_in,
        b_out,
        tower_in,
        line(tower_bias),
        line(tower_out),
        line(tower_end),
        behaviour,
        w_in,
        w_out,
    )
    (
        out_grad,
        in_grad,
        field_grad,
        seq_grad,
        proj,
        tower,
        predictions,
        b_proj_grad,
        gain,
        shift,
        tower_b,
        tower_o,
        tower_e,
        roots,
        gate,
        in_b,
        out_b,
        query,
        key,
        value,
    ) = place(*results)
    return (
        predictions,
        field_grad,
        seq_grad,
        query,
        key,
        value,
        proj,
        b_proj_grad,
        gain,
        shift,
        gate.transpose(1, 2, 0),
        in_grad,
        in_b.transpose(1, 0, 2),
        out_grad,
        out_b.transpose(1, 0, 2),
        tower,
        tower_b,
        tower_o,
        tower_e,
        roots,
    )


def solution(mesh):
    each = (P("dp", None), P("dp", None), P("dp"), P("dp"), P("dp"), P("dp"))
    ranks = (2, 3, 3, 3, 3, 3, 3, 2, 2, 2, 3, 4, 3, 4, 3, 3, 2, 2, 2, 2)
    outs = tuple(
        P("section", "dp", *(None,) * (rank - 2)) if i < 3 else P("section", *(None,) * (rank - 1))
        for i, rank in enumerate(ranks)
    )
    return jax.shard_map(
        body, mesh=mesh, in_specs=each + (P(),) * 16, out_specs=outs, check_vma=False
    )
```

profile of v0, /device:TPU:65, one launch (start us, length us, event | category | flops | bytes accessed | tf_op | source)
XLA Modules:
  0.0 103.9 jit_solution(11490495155791607597)
XLA Ops:
  0.7 91.7 %rank_and_sum.1 = (bf16[25,2,1024,128]{3,2,1,0:T(8,128)(2,1)S(1)}, bf16[5,2,256,128]{3,2,1,0:T(8,128)(2,1)S(1)}, f32[1,2,128,128]{3,2,1,0:T(8,128)S(1)}, f32[24,...) custom-call(bf16[256,640]{1,0:T(8,128)(2,1)} %fields.1, ...), custom_call_target="tpu_custom_call" | custom-call | tf_op jit(solution)/shard_map/rank_and_sum/pallas_call | solution.py:883
  92.3 11.3 %place.1 = (f32[1,6,1024,512]{3,2,1,0:T(8,128)}, f32[1,6,512,1024]{3,2,1,0:T(8,128)}, f32[1,256,640]{2,1,0:T(8,128)}, f32[1,256,3200]{2,1,0:T(8,128)}, f32[1,640...) custom-call(bf16[25,2,1024,128]{3,2,1,0:T(8,128)(2,1)S(1)} %get-tupl, ...), custom_call_target="tpu_custom_call" | custom-call | tf_op jit(solution)/shard_map/place/pallas_call | solution.py:1051
where the time goes:
time: 104 us
  Pallas kernels  103 us (99%)
    pallas_call x1, Pallas kernels, run(): pl.pallas_call(kernel, out_shape=outs, in_specs=[here] * 19 + [far] * 3,...  91.7 us
    pallas_call x1, Pallas kernels, place(): pl.pallas_call(place_kernel, out_shape=[jax.ShapeDtypeStruct(shape, F32)...  11.3 us

commit v1 on v0

--- a/solution.py
+++ b/solution.py
@@ -25,7 +25,8 @@
 PIECES = tuple((at, SPAN) for at in range(0, 3072, SPAN)) + ((3072, LANES),)
 PROJ_ROWS = 256
 SMALL_ROWS = 128
-BLOCK = 64
+BLOCK = 128
+BACK_BLOCK = 64
 
 
 def coords():
@@ -159,8 +160,11 @@
         region = self.total(unit, self.span(self.start_of(unit % DIMS, k + 1), size))
         return self.remote(unit, DIMS + 1 + k, region, region, neighbour((unit + k) % DIMS))
 
-    def back(self, unit):
-        return self.remote(unit, DIMS + 1 + HALVINGS, self.total(unit), self.total(unit), sibling())
+    def back(self, unit, late):
+        size = self.rows // 2
+        own = which_half(unit % DIMS)
+        region = self.total(unit, self.span((own + late * (1 - 2 * own)) * size, size))
+        return self.remote(unit, DIMS + 1 + HALVINGS, region, region, sibling())
 
     def send(self, group, unit, halves):
         for i, rows in enumerate(halves):
@@ -236,8 +240,8 @@
             def one(unit):
                 if k > 0:
                     self.spread(unit, k - 1).start()
-                else:
-                    self.back(unit).start()
+                if k < 2:
+                    self.back(unit, 1 - k).start()
 
             self.each(base, count, one)
         else:
@@ -280,20 +284,21 @@
 
 
 PLAN_FIRST = (
-    ("ins", 1, 6), ("back", 0, 1), ("sum", 3, 0), ("front",), ("sum", 3, 1), ("sum", 4, 0), ("send_p",), ("sum", 3, 2),
-    ("sum", 4, 1), ("take_p",), ("sum", 3, 3), ("sum", 4, 2), ("sum", 3, 4), ("sum", 4, 3), ("sum_p", 0), ("sum", 4, 4),
-    ("sum_p", 1), ("seq", 0, 2), ("sum_p", 2), ("seq", 2, 4), ("sum_p", 3), ("weights",), ("tiny", 0), ("sum_p", 4),
-    ("tiny", 1), ("all_p", 1), ("tiny", 2), ("all_p", 2), ("tiny", 3), ("all_p", 3), ("tiny", 4), ("all_p", 4),
-    ("tiny", 5), ("tiny", 6),
+    ("ins", 1, 6), ("back", 0, 1), ("front",), ("sum", 3, 0), ("sum", 4, 0), ("send_p",), ("sum", 3, 1), ("take_p",),
+    ("sum", 4, 1), ("sum", 3, 2), ("sum", 4, 2), ("sum", 3, 3), ("sum_p", 0), ("sum", 3, 4), ("sum", 4, 3),
+    ("sum_p", 1), ("seq", 0, 1), ("sum", 4, 4), ("sum_p", 2), ("seq", 1, 2), ("weights",), ("tiny", 0), ("sum_p", 3),
+    ("sum_p", 4), ("tiny", 1), ("tiny", 2), ("all_p", 1), ("tiny", 3), ("all_p", 2), ("tiny", 4), ("all_p", 3),
+    ("tiny", 5), ("all_p", 4), ("tiny", 6),
 )
 PLAN_SECOND = (
-    ("outs", 0, 6), ("tower",), ("ins", 0, 1), ("sum", 0, 0), ("back", 1, 3), ("sum", 1, 0), ("sum", 0, 1),
-    ("back", 3, 6), ("sum", 0, 2), ("sum", 1, 1), ("sum", 2, 0), ("front",), ("sum", 0, 3), ("sum", 1, 2), ("sum", 2, 1),
-    ("send_v",), ("sum", 0, 4), ("sum", 1, 3), ("sum", 2, 2), ("take_v",), ("all", 0, 1), ("sum", 1, 4), ("sum", 2, 3),
-    ("sum_v", 0), ("all", 0, 2), ("all", 1, 1), ("sum", 2, 4), ("sum_v", 1), ("all", 3, 0), ("all", 0, 3), ("all", 1, 2),
-    ("all", 2, 1), ("sum_v", 2), ("all", 3, 1), ("all", 4, 0), ("all", 1, 3), ("all", 2, 2), ("sum_v", 3), ("all", 0, 4),
-    ("all", 3, 2), ("all", 4, 1), ("sum_v", 4), ("all", 2, 3), ("all", 1, 4), ("all_v", 1), ("all", 3, 3), ("all", 4, 2),
-    ("all_v", 2), ("all", 2, 4), ("all", 4, 3), ("all_v", 3), ("all", 3, 4), ("all_v", 4), ("all", 4, 4),
+    ("outs", 0, 6), ("send_t", 0), ("back", 0, 1), ("send_i", 0), ("sum", 0, 0), ("take_t", 0), ("take_i", 0),
+    ("sum", 1, 0), ("back", 3, 6), ("sum", 0, 1), ("back", 1, 3), ("sum", 1, 1), ("sum", 2, 0), ("sum", 0, 2),
+    ("front",), ("sum", 1, 2), ("send_v",), ("sum", 2, 1), ("sum", 0, 3), ("take_v",), ("sum", 1, 3), ("sum", 2, 2),
+    ("sum", 0, 4), ("sum_v", 0), ("sum", 1, 4), ("sum", 2, 3), ("sum_v", 1), ("all", 0, 1), ("all", 1, 1),
+    ("sum", 2, 4), ("sum_v", 2), ("all", 3, 0), ("all", 0, 2), ("all", 3, 1), ("sum_v", 3), ("all", 4, 0),
+    ("all", 2, 1), ("all", 1, 2), ("sum_v", 4), ("all", 4, 1), ("all", 2, 2), ("all_v", 1), ("all", 4, 2),
+    ("all_v", 2), ("all", 1, 3), ("all", 3, 2), ("all", 0, 3), ("all_v", 3), ("all", 4, 3), ("all_v", 4),
+    ("all", 2, 3), ("all", 1, 4), ("all", 3, 3), ("all", 0, 4), ("all", 2, 4), ("all", 4, 4), ("all", 3, 4),
 )
 
 
@@ -345,8 +350,9 @@
     square = v * v
     bent = jnp.tanh(v * (ROOT + ROOT * CUBE * square))
     half = 0.5 + 0.5 * bent
-    slope = half + 0.5 * v * (1.0 - bent * bent) * (ROOT + 3.0 * ROOT * CUBE * square)
-    return v * half, slope
+    value = v * half
+    slope = half + value * (1.0 - half) * (2.0 * ROOT + 6.0 * ROOT * CUBE * square)
+    return value, slope
 
 
 def column_sum(array):
@@ -528,8 +534,8 @@
     def front_forward():
         projected = product(joined[...], proj_turned[...]) + b_proj[...]
         act, slope_proj = gelu_both(projected)
+        activation[...] = act.astype(BF16)
         act = act.astype(BF16).astype(F32)
-        activation[...] = act
         proj_slope[...] = slope_proj
         centred = act - row_sum(act) * (1.0 / HIDDEN)
         scale = lax.rsqrt(row_sum(centred * centred) * (1.0 / HIDDEN) + EPSILON)
@@ -559,8 +565,6 @@
         d_residual[...] = jnp.zeros_like(d_residual)
 
     def expert_forward(e, _):
-        load_in(e).wait()
-        load_out(e).wait()
         pre = product(normed[...], w_in[e]) + b_in[pl.ds(e, 1)]
         out, grade = gelu_both(pre)
         active[e] = out.astype(BF16)
@@ -573,7 +577,7 @@
 
     def tower_both():
         branch = d_residual[...]
-        residual = activation[...] + branch
+        residual = activation[...].astype(F32) + branch
         in_first = info[:, 1:2] == 0.0
         valid = info[:, 2:3]
         residual_low[...] = residual.astype(BF16)
@@ -650,7 +654,7 @@
         d_proj_low[...] = low
 
     def attention_back(block):
-        rows = pl.ds(pl.multiple_of(block * BLOCK, BLOCK), BLOCK)
+        rows = pl.ds(pl.multiple_of(block * BACK_BLOCK, BACK_BLOCK), BACK_BLOCK)
         probe, attn = attention(rows)
         pooled_rows[rows] = exact(pool(rows, attn), pooled_w[...])
         d_joined = contract_cols(d_proj_low[rows], proj_turned[...])
@@ -726,7 +730,15 @@
         prepare()
         lax.fori_loop(0, ROWS // BLOCK, attention_forward, 0)
         front_forward()
-        lax.fori_loop(0, EXPERTS, expert_forward, 0)
+        for e in range(EXPERTS):
+            load_in(e).wait()
+            load_out(e).wait()
+
+        @pl.loop(0, EXPERTS, step=2)
+        def _(e):
+            expert_forward(e, 0)
+            expert_forward(e + 1, 0)
+
         tower_both()
         d_normed[...] = jnp.zeros_like(d_normed)
         d_mixing[...] = jnp.zeros_like(d_mixing)
@@ -764,14 +776,13 @@
                 def _():
                     big.take(5 + e, IN_UNIT + 2 * e - 2, in_halves(e - 1, core))
 
-        def tower():
-            big.send(12, TOWER_UNIT, tower_halves(1 - core))
-            big.take(12, TOWER_UNIT, tower_halves(core))
-
         work = {
             "outs": outs,
             "ins": ins,
-            "tower": tower,
+            "send_t": lambda e: big.send(12, TOWER_UNIT, tower_halves(1 - core)),
+            "take_t": lambda e: big.take(12, TOWER_UNIT, tower_halves(core)),
+            "send_i": lambda e: big.send(6 + e, IN_UNIT + 2 * e, in_halves(e, 1 - core)),
+            "take_i": lambda e: big.take(6 + e, IN_UNIT + 2 * e, in_halves(e, core)),
             "back": backs,
             "front": front_backward,
             "sum": lambda c, step: big.reduce(DIMS * c, DIMS, step),
@@ -791,7 +802,7 @@
             PLAN_FIRST,
             big,
             {
-                "seq": lambda start, end: pl.loop(start, end)(attention_back),
+                "seq": lambda start, end: pl.loop(2 * start, 2 * end)(attention_back),
                 "weights": attention_weights,
                 "send_p": lambda: proj.send(0, 0, proj_half(1 - core)),
                 "take_p": lambda: proj.take(0, 0, proj_half(core)),
@@ -845,7 +856,7 @@
         keep(16, HIDDEN, dtype=BF16),
         keep(ROWS, 8),
         keep(ROWS, FIELDS, dtype=BF16),
-        keep(ROWS, HIDDEN),
+        keep(ROWS, HIDDEN, dtype=BF16),
         keep(ROWS, HIDDEN),
         keep(ROWS, HIDDEN, dtype=BF16),
         keep(ROWS, HIDDEN),

time: 104 us -> 94.7 us (0.911)
  Pallas kernels: 103 us -> 93.7 us
    pallas_call x1, Pallas kernels: 91.7 us -> 82.3 us  [run(): pl.pallas_call(kernel, out_shape=outs, in_specs=[here] * 19 + [far] * 3,...]
where the time goes in v1:
time: 94.7 us; the launch traced here: 94.5 us
  Pallas kernels  93.7 us (99%)
    pallas_call x1, Pallas kernels, run(): pl.pallas_call(kernel, out_shape=outs, in_specs=[here] * 19 + [far] * 3,...  82.3 us
    pallas_call x1, Pallas kernels, place(): pl.pallas_call(place_kernel, out_shape=[jax.ShapeDtypeStruct(shape, F32)...  11.3 us

profile of v1, /device:TPU:65, one launch (start us, length us, event | category | flops | bytes accessed | tf_op | source)
XLA Modules:
  0.0 94.5 jit_solution(18402370814916717657)
XLA Ops:
  0.7 82.3 %rank_and_sum.1 = (bf16[25,2,1024,128]{3,2,1,0:T(8,128)(2,1)S(1)}, bf16[5,2,256,128]{3,2,1,0:T(8,128)(2,1)S(1)}, f32[1,2,128,128]{3,2,1,0:T(8,128)S(1)}, f32[24,...) custom-call(bf16[256,640]{1,0:T(8,128)(2,1)} %fields.1, ...), custom_call_target="tpu_custom_call" | custom-call | tf_op jit(solution)/shard_map/rank_and_sum/pallas_call | solution.py:894
  83.0 11.3 %place.1 = (f32[1,6,1024,512]{3,2,1,0:T(8,128)}, f32[1,6,512,1024]{3,2,1,0:T(8,128)}, f32[1,256,640]{2,1,0:T(8,128)}, f32[1,256,3200]{2,1,0:T(8,128)}, f32[1,640...) custom-call(bf16[25,2,1024,128]{3,2,1,0:T(8,128)(2,1)S(1)} %get-tupl, ...), custom_call_target="tpu_custom_call" | custom-call | tf_op jit(solution)/shard_map/place/pallas_call | solution.py:1062

commit v2 on v1

--- a/solution.py
+++ b/solution.py
@@ -85,7 +85,6 @@
         (
             self.kept,
             self.arrived,
-            self.doubled,
             self.pair_send,
             self.pair_recv,
             self.send_sem,
@@ -142,12 +141,15 @@
 
     def double(self, unit, j):
         local = unit - self.first
-        src = self.kept.at[local, self.own_share(unit)] if j == 0 else self.doubled.at[local, j - 1]
+        start = self.rows - self.share + j * self.share
+        src = self.kept.at[local, self.own_share(unit)]
+        if j:
+            src = self.arrived.at[local, pl.ds(start - self.share, self.share)]
         return self.remote(
             unit,
             HALVINGS + j,
             src,
-            self.arrived.at[local, pl.ds(self.rows - self.share + j * self.share, self.share)],
+            self.arrived.at[local, pl.ds(start, self.share)],
             neighbour((unit + HALVINGS + j) % DIMS),
         )
 
@@ -214,10 +216,11 @@
                 return
             j = step - HALVINGS
             region = self.own_share(unit)
-            old = self.kept[here, region] if j == 0 else self.doubled[here, j - 1]
+            before = pl.ds(self.rows - size + (j - 1) * size, size)
+            old = self.arrived[here, before] if j else self.kept[here, region]
             new = (old.astype(F32) + came).astype(dtype)
             if step + 1 < DIMS:
-                self.doubled[here, j] = new
+                self.arrived[here, arrivals] = new
                 self.double(unit, j + 1).start()
             else:
                 self.out[unit, coords()[3], region] = new
@@ -268,7 +271,6 @@
     return [
         pltpu.VMEM((reduced, rows, LANES), dtype),
         pltpu.VMEM((reduced, rows - share + (DIMS - HALVINGS) * share, LANES), dtype),
-        pltpu.VMEM((reduced, max(1, DIMS - HALVINGS - 1), share, LANES), dtype),
         pltpu.SemaphoreType.DMA((groups,)),
         pltpu.SemaphoreType.DMA((groups,)),
         pltpu.SemaphoreType.DMA((SLOTS,)),
@@ -375,7 +377,6 @@
 
 
 def kernel(
-    fields,
     lengths,
     domains,
     validity,
@@ -383,17 +384,18 @@
     w_query,
     w_key,
     w_value,
-    w_proj,
     b_proj,
     norm_gain,
     norm_shift,
     gate_turned,
     b_in,
     b_out,
-    tower_in,
     tower_bias,
     tower_out,
     tower_end,
+    fields_hbm,
+    w_proj_hbm,
+    tower_in_hbm,
     behaviour_hbm,
     w_in_hbm,
     w_out_hbm,
@@ -404,6 +406,8 @@
     pred_all,
     d_fields,
     d_seq,
+    fields,
+    tower_in,
     behaviour,
     w_in,
     w_out,
@@ -453,21 +457,28 @@
     for other in (sibling(), cross()):
         pl.semaphore_signal(barrier, inc=1, device_id=other, device_id_type=MESH)
 
-    seq_copy = pltpu.make_async_copy(behaviour_hbm, behaviour, load_sem.at[12])
-
-    def load_in(e):
-        return pltpu.make_async_copy(w_in_hbm.at[e], w_in.at[e], load_sem.at[e])
-
-    def load_out(e):
-        return pltpu.make_async_copy(w_out_hbm.at[e], w_out.at[e], load_sem.at[6 + e])
+    seq_copy = pltpu.make_async_copy(behaviour_hbm, behaviour, load_sem.at[2])
+
+    load_in = pltpu.make_async_copy(w_in_hbm, w_in, load_sem.at[0])
+    load_out = pltpu.make_async_copy(w_out_hbm, w_out, load_sem.at[1])
+    load_fields = pltpu.make_async_copy(fields_hbm, fields, load_sem.at[3])
+    load_tower = pltpu.make_async_copy(tower_in_hbm, tower_in, load_sem.at[4])
+    cut = FIELDS - EMBED
+    load_proj = [
+        pltpu.make_async_copy(w_proj_hbm.at[pl.ds(cut, EMBED)], proj_turned.at[pl.ds(0, EMBED)], load_sem.at[5]),
+        pltpu.make_async_copy(w_proj_hbm.at[pl.ds(0, cut)], proj_turned.at[pl.ds(EMBED, cut)], load_sem.at[6]),
+    ]
 
     tile = lane_match(EMBED, SPAN, EMBED)
 
     def prepare():
         seq_copy.start()
-        for e in range(EXPERTS):
-            load_in(e).start()
-            load_out(e).start()
+        load_fields.start()
+        for copy in load_proj:
+            copy.start()
+        load_in.start()
+        load_out.start()
+        load_tower.start()
         group = lax.broadcasted_iota(jnp.int32, (SPAN, SPAN), 0) // EMBED
         groups[...] = (group == lanes((SPAN, SPAN)) // EMBED).astype(F32).astype(BF16)
         eye = lane_match(EMBED, LANES, 0)
@@ -476,8 +487,6 @@
         pooled_w[...] = exact_rows(tile, eye)
         back_w[...] = exact_rows(w_value[...], tile)
         target_w[...] = exact_rows(tile, exact(exact_cols(w_key[...], w_query[...]), eye))
-        proj_turned[:EMBED] = w_proj[FIELDS - EMBED :]
-        proj_turned[EMBED:] = w_proj[: FIELDS - EMBED]
         rows = [lengths[...].astype(F32), domains[...].astype(F32), validity[...].astype(F32), cotangent[...]]
         info[...] = jnp.transpose(jnp.concatenate(rows + [jnp.zeros((4, ROWS), F32)], axis=0))
         gate_rows[...] = jnp.zeros_like(gate_rows)
@@ -485,6 +494,7 @@
         small[...] = jnp.zeros_like(small)
         tiny[0] = jnp.zeros((TINY_ROWS, LANES), F32)
         seq_copy.wait()
+        load_fields.wait()
 
     def group_sum(value, terms):
         count, width = value.shape
@@ -532,6 +542,8 @@
         return [gates[:, i : i + 1] for i in range(6)]
 
     def front_forward():
+        for copy in load_proj:
+            copy.wait()
         projected = product(joined[...], proj_turned[...]) + b_proj[...]
         act, slope_proj = gelu_both(projected)
         activation[...] = act.astype(BF16)
@@ -576,6 +588,7 @@
         return 0
 
     def tower_both():
+        load_tower.wait()
         branch = d_residual[...]
         residual = activation[...].astype(F32) + branch
         in_first = info[:, 1:2] == 0.0
@@ -730,9 +743,8 @@
         prepare()
         lax.fori_loop(0, ROWS // BLOCK, attention_forward, 0)
         front_forward()
-        for e in range(EXPERTS):
-            load_in(e).wait()
-            load_out(e).wait()
+        load_in.wait()
+        load_out.wait()
 
         @pl.loop(0, EXPERTS, step=2)
         def _(e):
@@ -742,12 +754,11 @@
         tower_both()
         d_normed[...] = jnp.zeros_like(d_normed)
         d_mixing[...] = jnp.zeros_like(d_mixing)
-        lax.fori_loop(0, EXPERTS, spread_residual, 0)
         pl.semaphore_wait(barrier, 7)
 
     def family(i, first=0, to_other=False):
         out = (big_out, proj_out, small_out)[i]
-        return Family(FAMILIES[i][3], out, family_refs[7 * i : 7 * i + 7], first, to_other)
+        return Family(FAMILIES[i][3], out, family_refs[6 * i : 6 * i + 6], first, to_other)
 
     def perform(plan, big, extra):
         def backs(start, end):
@@ -758,6 +769,7 @@
             def _(e):
                 @pl.when(e < end)
                 def _():
+                    spread_residual(e, 0)
                     big.send(e, 2 * e, out_halves(e, 1 - core))
 
                 @pl.when(e > start)
@@ -769,6 +781,7 @@
             def _(e):
                 @pl.when(e < end)
                 def _():
+                    spread_residual(e, 0)
                     expert_backward(e, 0)
                     big.send(6 + e, IN_UNIT + 2 * e, in_halves(e, 1 - core))
 
@@ -796,6 +809,7 @@
 
     @pl.when(section == 0)
     def _():
+        spread_residual(0, 0)
         big = family(0, SPLIT, True)
         proj = family(1)
         perform(
@@ -843,6 +857,8 @@
         return pltpu.VMEM(shape, dtype)
 
     scratch = [
+        keep(ROWS, FIELDS, dtype=BF16),
+        keep(HIDDEN, HIDDEN, dtype=BF16),
         keep(ROWS, SEQ, dtype=BF16),
         keep(EXPERTS, HIDDEN, WIDE, dtype=BF16),
         keep(EXPERTS, WIDE, HIDDEN, dtype=BF16),
@@ -878,7 +894,7 @@
         keep(64, HIDDEN),
         keep(DIMS + 2, TINY_ROWS, LANES),
         keep(DIMS + 1, TINY_ROWS, LANES),
-        pltpu.SemaphoreType.DMA((13,)),
+        pltpu.SemaphoreType.DMA((7,)),
         pltpu.SemaphoreType.DMA((DIMS + 1,)),
         pltpu.SemaphoreType.DMA((DIMS + 1,)),
     ]
@@ -894,7 +910,7 @@
     return pl.pallas_call(
         kernel,
         out_shape=outs,
-        in_specs=[here] * 19 + [far] * 3,
+        in_specs=[here] * 16 + [far] * 6,
         out_specs=[here] * 7,
         scratch_shapes=scratch,
         compiler_params=pltpu.CompilerParams(
@@ -902,6 +918,10 @@
         ),
         name="rank_and_sum",
     )(*args)
+
+
+SMALL_SHAPES = ((1, ROWS),) + ((1, 512),) * 5 + ((1, 2),) * 2
+SMALL_SHAPES += ((7, 1, 512), (6, 1, 1024), (6, 1, 512)) + ((1, 16, 16),) * 3
 
 
 def place_kernel(
@@ -918,38 +938,30 @@
     seq_grad,
     proj,
     tower,
-    predictions,
-    b_proj,
-    gain,
-    shift,
-    tower_b,
-    tower_o,
-    tower_e,
-    roots,
-    gate,
-    in_b,
-    out_b,
-    query,
-    key,
-    value,
-    out_stage,
-    in_stage,
-    seq_stage,
-    field_stage,
-    proj_stage,
-    tower_stage,
-    out_sem,
-    in_sem,
-    other_sem,
+    *rest,
 ):
+    count = len(SMALL_SHAPES)
+    small_outs, small_stages = rest[:count], rest[count : 2 * count]
+    (
+        out_stage,
+        in_stage,
+        seq_stage,
+        field_stage,
+        proj_stage,
+        tower_stage,
+        out_sem,
+        in_sem,
+        other_sem,
+        small_sem,
+    ) = rest[2 * count :]
     section = lax.axis_index("section")
     second = (section == 1).astype(F32)
 
     def out_copy(e, slot):
-        return pltpu.make_async_copy(out_stage.at[slot], out_grad.at[0, e], out_sem.at[e])
+        return pltpu.make_async_copy(out_stage.at[slot], out_grad.at[0, e], out_sem.at[slot])
 
     def in_copy(e, slot):
-        return pltpu.make_async_copy(in_stage.at[slot], in_grad.at[0, e], in_sem.at[e])
+        return pltpu.make_async_copy(in_stage.at[slot], in_grad.at[0, e], in_sem.at[slot])
 
     stages = ((seq_stage, seq_grad), (field_stage, field_grad), (proj_stage, proj), (tower_stage, tower))
     others = [pltpu.make_async_copy(stage, grad.at[0], other_sem.at[i]) for i, (stage, grad) in enumerate(stages)]
@@ -959,8 +971,8 @@
         out_stage[0] = jnp.zeros((WIDE, HIDDEN), F32)
         in_stage[0] = jnp.zeros((HIDDEN, WIDE), F32)
         for e in range(EXPERTS):
-            out_copy(e, 0).start()
-            in_copy(e, 0).start()
+            pltpu.make_async_copy(out_stage.at[0], out_grad.at[0, e], out_sem.at[2 + e]).start()
+            pltpu.make_async_copy(in_stage.at[0], in_grad.at[0, e], in_sem.at[2 + e]).start()
         seq_stage[...] = seq_rows[...].astype(F32)
         others[0].start()
         field_stage[...] = field_rows[...]
@@ -973,12 +985,14 @@
         others[2].start()
         tower_stage[...] = jnp.zeros_like(tower_stage)
         others[3].start()
-        for e in range(EXPERTS):
-            out_copy(e, 0).wait()
-            in_copy(e, 0).wait()
 
     @pl.when(section == 1)
     def _():
+        field_stage[...] = jnp.zeros_like(field_stage)
+        others[1].start()
+        proj_stage[...] = jnp.zeros_like(proj_stage)
+        others[2].start()
+
         @pl.loop(0, EXPERTS)
         def _(e):
             slot = e % 2
@@ -1005,19 +1019,33 @@
                         in_stage[slot, :, at : at + LANES] = big[IN_UNIT + 2 * e + j, core, rows].astype(F32)
             in_copy(e, slot).start()
 
+            @pl.when(e == 0)
+            def _():
+                seq_stage[...] = jnp.zeros_like(seq_stage)
+                others[0].start()
+
         for core in range(2):
             for j in range(2):
                 at = slice((2 * core + j) * LANES, (2 * core + j + 1) * LANES)
                 tower_stage[:, at] = big[TOWER_UNIT, core, j * HIDDEN : (j + 1) * HIDDEN].astype(F32)
-        seq_stage[...] = jnp.zeros_like(seq_stage)
-        field_stage[...] = jnp.zeros_like(field_stage)
-        proj_stage[...] = jnp.zeros_like(proj_stage)
-        for other in others:
-            other.start()
-        for e in (EXPERTS - 2, EXPERTS - 1):
-            out_copy(e, e % 2).wait()
-            in_copy(e, e % 2).wait()
-
+        others[3].start()
+
+    (
+        predictions,
+        b_proj,
+        gain,
+        shift,
+        tower_b,
+        tower_o,
+        tower_e,
+        roots,
+        gate,
+        in_b,
+        out_b,
+        query,
+        key,
+        value,
+    ) = small_stages
     for j in range(2):
         predictions[:, j * LANES : (j + 1) * LANES] = jnp.where(section == 1, pred_all[j, 0:1], 0.0)
 
@@ -1034,9 +1062,9 @@
     tower_b[...] = head[3:4]
     tower_o[...] = head[4:5]
     tower_e[...] = head[5:6, 0:2]
-    count = head[5:6, 4:5]
-    squares = head[5:6, 2:4] / (float(HIDDEN) * jnp.maximum(count, 1.0)) + EPSILON
-    roots[...] = jnp.where(count > 0.0, jnp.sqrt(squares), 0.0) * second
+    valid = head[5:6, 4:5]
+    squares = head[5:6, 2:4] / (float(HIDDEN) * jnp.maximum(valid, 1.0)) + EPSILON
+    roots[...] = jnp.where(valid > 0.0, jnp.sqrt(squares), 0.0) * second
     gate_lines, out_lines = rows(8, 8), rows(32, 8)
     in_lines = jnp.concatenate([rows(16, 8), rows(24, 8)], axis=1)
     for i in range(7):
@@ -1049,31 +1077,51 @@
     query[0] = three[:EMBED, 0:16]
     key[0] = three[:EMBED, 16:32]
     value[0] = three[:EMBED, 32:48]
-    for other in others:
-        other.wait()
+    smalls = [
+        pltpu.make_async_copy(stage, out, small_sem.at[i])
+        for i, (stage, out) in enumerate(zip(small_stages, small_outs))
+    ]
+    for copy in smalls:
+        copy.start()
+
+    @pl.when(section == 0)
+    def _():
+        for e in range(EXPERTS):
+            pltpu.make_async_copy(out_stage.at[0], out_grad.at[0, e], out_sem.at[2 + e]).wait()
+            pltpu.make_async_copy(in_stage.at[0], in_grad.at[0, e], in_sem.at[2 + e]).wait()
+
+    @pl.when(section == 1)
+    def _():
+        for e in (EXPERTS - 2, EXPERTS - 1):
+            out_copy(e, e % 2).wait()
+            in_copy(e, e % 2).wait()
+
+    for copy in others + smalls:
+        copy.wait()
 
 
 def place(*results):
     here = pl.BlockSpec(memory_space=pltpu.VMEM)
     far = pl.BlockSpec(memory_space=pl.ANY)
     shapes = [(1, 6, 1024, 512), (1, 6, 512, 1024), (1, ROWS, FIELDS), (1, ROWS, SEQ), (1, 640, 512), (1, 512, 512)]
-    shapes += [(1, ROWS)] + [(1, 512)] * 5 + [(1, 2)] * 2
-    shapes += [(7, 1, 512), (6, 1, 1024), (6, 1, 512)] + [(1, 16, 16)] * 3
+    shapes += SMALL_SHAPES
     return pl.pallas_call(
         place_kernel,
         out_shape=[jax.ShapeDtypeStruct(shape, F32) for shape in shapes],
         in_specs=[here] * 7,
-        out_specs=[far] * 6 + [here] * 14,
-        scratch_shapes=[
+        out_specs=[far] * 20,
+        scratch_shapes=[pltpu.VMEM(shape, F32) for shape in SMALL_SHAPES]
+        + [
             pltpu.VMEM((2, WIDE, HIDDEN), F32),
             pltpu.VMEM((2, HIDDEN, WIDE), F32),
             pltpu.VMEM((ROWS, SEQ), F32),
             pltpu.VMEM((ROWS, FIELDS), F32),
             pltpu.VMEM((FIELDS, HIDDEN), F32),
             pltpu.VMEM((HIDDEN, HIDDEN), F32),
-            pltpu.SemaphoreType.DMA((EXPERTS,)),
-            pltpu.SemaphoreType.DMA((EXPERTS,)),
+            pltpu.SemaphoreType.DMA((2 + EXPERTS,)),
+            pltpu.SemaphoreType.DMA((2 + EXPERTS,)),
             pltpu.SemaphoreType.DMA((4,)),
+            pltpu.SemaphoreType.DMA((len(SMALL_SHAPES),)),
         ],
         compiler_params=pltpu.CompilerParams(vmem_limit_bytes=24 << 20),
         name="place",
@@ -1108,7 +1156,6 @@
         return array.reshape(1, -1)
 
     results = run(
-        fields,
         line(lengths),
         line(domains),
         line(validity),
@@ -1116,17 +1163,18 @@
         w_query,
         w_key,
         w_value,
-        w_proj,
         line(b_proj),
         line(norm_gain),
         line(norm_shift),
         gate_weight.T,
         b_in,
         b_out,
-        tower_in,
         line(tower_bias),
         line(tower_out),
         line(tower_end),
+        fields,
+        w_proj,
+        tower_in,
         behaviour,
         w_in,
         w_out,

time: 94.7 us -> 92.8 us (0.980)
  Pallas kernels: 93.7 us -> 91.7 us
    pallas_call x1, Pallas kernels: 82.3 us -> 81.1 us  [run(): pl.pallas_call(kernel, out_shape=outs, in_specs=[here] * 16 + [far] * 6,...]
where the time goes in v2:
time: 92.8 us; the launch traced here: 92.6 us
  Pallas kernels  91.7 us (99%)
    pallas_call x1, Pallas kernels, run(): pl.pallas_call(kernel, out_shape=outs, in_specs=[here] * 16 + [far] * 6,...  81.1 us
    pallas_call x1, Pallas kernels, place(): pl.pallas_call(place_kernel, out_shape=[jax.ShapeDtypeStruct(shape, F32)...  10.7 us

profile of v2, /device:TPU:65, one launch (start us, length us, event | category | flops | bytes accessed | tf_op | source)
XLA Modules:
  0.0 92.6 jit_solution(10262783112410601358)
XLA Ops:
  0.7 81.1 %rank_and_sum.1 = (bf16[25,2,1024,128]{3,2,1,0:T(8,128)(2,1)S(1)}, bf16[5,2,256,128]{3,2,1,0:T(8,128)(2,1)S(1)}, f32[1,2,128,128]{3,2,1,0:T(8,128)S(1)}, f32[24,...) custom-call(s32[1,256]{1,0:T(1,128)} %bitcast.20, ...), custom_call_target="tpu_custom_call" | custom-call | tf_op jit(solution)/shard_map/rank_and_sum/pallas_call | solution.py:910
  81.7 10.7 %place.1 = (f32[1,6,1024,512]{3,2,1,0:T(8,128)}, f32[1,6,512,1024]{3,2,1,0:T(8,128)}, f32[1,256,640]{2,1,0:T(8,128)}, f32[1,256,3200]{2,1,0:T(8,128)}, f32[1,640...) custom-call(bf16[25,2,1024,128]{3,2,1,0:T(8,128)(2,1)S(1)} %get-tupl, ...), custom_call_target="tpu_custom_call" | custom-call | tf_op jit(solution)/shard_map/place/pallas_call | solution.py:1108

commit v3 on v2

--- a/solution.py
+++ b/solution.py
@@ -76,12 +76,14 @@
 
 
 class Family:
-    def __init__(self, rows, out, refs, first, to_other=False):
+    def __init__(self, rows, out, refs, first, here, to_other=False, unrolled=False):
         self.rows = rows
         self.share = rows >> HALVINGS
         self.out = out
         self.first = first
         self.to_other = to_other
+        self.unrolled = unrolled
+        self.sides, self.neighbours, self.core, self.sibling, self.cross = here
         (
             self.kept,
             self.arrived,
@@ -91,8 +93,14 @@
             self.recv_sem,
         ) = refs
 
+    def side(self, dim):
+        return self.sides[dim] if isinstance(dim, int) else which_half(dim)
+
+    def neighbour(self, dim):
+        return self.neighbours[dim] if isinstance(dim, int) else neighbour(dim)
+
     def total(self, units, rows=slice(None)):
-        return self.out.at[units, coords()[3], rows]
+        return self.out.at[units, self.core, rows]
 
     def remote(self, unit, slot, src, dst, to):
         return pltpu.make_async_remote_copy(
@@ -107,7 +115,7 @@
     def start_of(self, part, step):
         start = 0
         for k in range(step):
-            start = start + which_half((part + k) % DIMS) * (self.rows >> (k + 1))
+            start = start + self.side((part + k) % DIMS) * (self.rows >> (k + 1))
         return start
 
     def span(self, start, size):
@@ -122,21 +130,21 @@
             dst_ref=self.kept.at[pl.ds(unit - self.first, count)],
             send_sem=self.pair_send.at[group],
             recv_sem=self.pair_recv.at[group],
-            device_id=sibling(),
+            device_id=self.sibling,
             device_id_type=MESH,
         )
 
     def halve(self, unit, k):
         size = self.rows >> (k + 1)
         dim = (unit + k) % DIMS
-        start = self.start_of(unit % DIMS, k) + (1 - which_half(dim)) * size
+        start = self.start_of(unit % DIMS, k) + (1 - self.side(dim)) * size
         local = unit - self.first
         return self.remote(
             unit,
             k,
             self.kept.at[local, self.span(start, size)],
             self.arrived.at[local, pl.ds(self.rows - 2 * size, size)],
-            neighbour(dim),
+            self.neighbour(dim),
         )
 
     def double(self, unit, j):
@@ -150,27 +158,27 @@
             HALVINGS + j,
             src,
             self.arrived.at[local, pl.ds(start, self.share)],
-            neighbour((unit + HALVINGS + j) % DIMS),
+            self.neighbour((unit + HALVINGS + j) % DIMS),
         )
 
     def over(self, unit):
         region = self.total(unit, self.own_share(unit))
-        return self.remote(unit, DIMS, region, region, cross())
+        return self.remote(unit, DIMS, region, region, self.cross)
 
     def spread(self, unit, k):
         size = self.rows >> (k + 1)
         region = self.total(unit, self.span(self.start_of(unit % DIMS, k + 1), size))
-        return self.remote(unit, DIMS + 1 + k, region, region, neighbour((unit + k) % DIMS))
+        return self.remote(unit, DIMS + 1 + k, region, region, self.neighbour((unit + k) % DIMS))
 
     def back(self, unit, late):
         size = self.rows // 2
-        own = which_half(unit % DIMS)
+        own = self.side(unit % DIMS)
         region = self.total(unit, self.span((own + late * (1 - 2 * own)) * size, size))
-        return self.remote(unit, DIMS + 1 + HALVINGS, region, region, sibling())
+        return self.remote(unit, DIMS + 1 + HALVINGS, region, region, self.sibling)
 
     def send(self, group, unit, halves):
         for i, rows in enumerate(halves):
-            self.out[unit + i, coords()[3]] = rows.astype(self.out.dtype)
+            self.out[unit + i, self.core] = rows.astype(self.out.dtype)
         self.across(group, unit, len(halves)).start()
 
     def take(self, group, unit, halves):
@@ -186,11 +194,27 @@
         pltpu.make_async_copy(ref, ref, self.recv_sem.at[base // DIMS, slot]).wait()
 
     def each(self, base, count, work):
+        if self.unrolled:
+            for i in range(count):
+                work(base + i)
+            return
+
         def one(i, _):
             work(base + i)
             return 0
 
         lax.fori_loop(0, count, one, 0)
+
+    def accumulate(self, here, to, start, size):
+        step = min(size, LANES)
+
+        def one(i, _):
+            rows = pl.ds(pl.multiple_of(to + i * step, step), step)
+            came = self.arrived[here, pl.ds(pl.multiple_of(start + i * step, step), step)]
+            self.kept[here, rows] = (self.kept[here, rows].astype(F32) + came.astype(F32)).astype(self.kept.dtype)
+            return 0
+
+        lax.fori_loop(0, size // step, one, 0)
 
     def reduce(self, base, count, step):
         dtype = self.kept.dtype
@@ -205,15 +229,14 @@
 
         def one(unit):
             here = unit - self.first
-            came = self.arrived[here, arrivals].astype(F32)
             if step < HALVINGS:
-                region = self.span(self.start_of(unit % DIMS, step + 1), size)
-                self.kept[here, region] = (self.kept[here, region].astype(F32) + came).astype(dtype)
+                self.accumulate(here, self.start_of(unit % DIMS, step + 1), arrivals.start, size)
                 if step + 1 < HALVINGS:
                     self.halve(unit, step + 1).start()
                 else:
                     self.double(unit, 0).start()
                 return
+            came = self.arrived[here, arrivals].astype(F32)
             j = step - HALVINGS
             region = self.own_share(unit)
             before = pl.ds(self.rows - size + (j - 1) * size, size)
@@ -223,7 +246,7 @@
                 self.arrived[here, arrivals] = new
                 self.double(unit, j + 1).start()
             else:
-                self.out[unit, coords()[3], region] = new
+                self.out[unit, self.core, region] = new
                 if self.to_other:
                     self.over(unit).start()
                 else:
@@ -248,7 +271,7 @@
 
             self.each(base, count, one)
         else:
-            self.await_chunk(DIMS + 1 + HALVINGS, base, self.out.at[units, 1 - coords()[3]])
+            self.await_chunk(DIMS + 1 + HALVINGS, base, self.out.at[units, 1 - self.core])
 
     def drain(self, reduced, gathered):
         def sent(slot, ref):
@@ -756,9 +779,17 @@
         d_mixing[...] = jnp.zeros_like(d_mixing)
         pl.semaphore_wait(barrier, 7)
 
-    def family(i, first=0, to_other=False):
+    here = (
+        [which_half(dim) for dim in range(DIMS)],
+        [neighbour(dim) for dim in range(DIMS)],
+        core,
+        sibling(),
+        cross(),
+    )
+
+    def family(i, first=0, to_other=False, unrolled=False):
         out = (big_out, proj_out, small_out)[i]
-        return Family(FAMILIES[i][3], out, family_refs[6 * i : 6 * i + 6], first, to_other)
+        return Family(FAMILIES[i][3], out, family_refs[6 * i : 6 * i + 6], first, here, to_other, unrolled)
 
     def perform(plan, big, extra):
         def backs(start, end):
@@ -810,8 +841,8 @@
     @pl.when(section == 0)
     def _():
         spread_residual(0, 0)
-        big = family(0, SPLIT, True)
-        proj = family(1)
+        big = family(0, SPLIT, True, True)
+        proj = family(1, unrolled=True)
         perform(
             PLAN_FIRST,
             big,
@@ -833,8 +864,8 @@
 
     @pl.when(section == 1)
     def _():
-        big = family(0)
-        vectors = family(2)
+        big = family(0, unrolled=True)
+        vectors = family(2, unrolled=True)
         perform(
             PLAN_SECOND,
             big,

time: 92.8 us -> 90.9 us (0.980)
  Pallas kernels: 91.7 us -> 89.9 us
    pallas_call x1, Pallas kernels: 81.1 us -> 79.2 us  [run(): pl.pallas_call(kernel, out_shape=outs, in_specs=[here] * 16 + [far] * 6,...]
where the time goes in v3:
time: 90.9 us; the launch traced here: 90.8 us
  Pallas kernels  89.9 us (99%)
    pallas_call x1, Pallas kernels, run(): pl.pallas_call(kernel, out_shape=outs, in_specs=[here] * 16 + [far] * 6,...  79.2 us
    pallas_call x1, Pallas kernels, place(): pl.pallas_call(place_kernel, out_shape=[jax.ShapeDtypeStruct(shape, F32)...  10.7 us

profile of v3, /device:TPU:65, one launch (start us, length us, event | category | flops | bytes accessed | tf_op | source)
XLA Modules:
  0.0 90.8 jit_solution(16661515057639400338)
XLA Ops:
  0.7 79.2 %rank_and_sum.1 = (bf16[25,2,1024,128]{3,2,1,0:T(8,128)(2,1)S(1)}, bf16[5,2,256,128]{3,2,1,0:T(8,128)(2,1)S(1)}, f32[1,2,128,128]{3,2,1,0:T(8,128)S(1)}, f32[24,...) custom-call(s32[1,256]{1,0:T(1,128)} %bitcast.20, ...), custom_call_target="tpu_custom_call" | custom-call | tf_op jit(solution)/shard_map/rank_and_sum/pallas_call | solution.py:941
  79.9 10.7 %place.1 = (f32[1,6,1024,512]{3,2,1,0:T(8,128)}, f32[1,6,512,1024]{3,2,1,0:T(8,128)}, f32[1,256,640]{2,1,0:T(8,128)}, f32[1,256,3200]{2,1,0:T(8,128)}, f32[1,640...) custom-call(bf16[25,2,1024,128]{3,2,1,0:T(8,128)(2,1)S(1)} %get-tupl, ...), custom_call_target="tpu_custom_call" | custom-call | tf_op jit(solution)/shard_map/place/pallas_call | solution.py:1139

commit v4 on v3

--- a/solution.py
+++ b/solution.py
@@ -309,21 +309,23 @@
 
 
 PLAN_FIRST = (
-    ("ins", 1, 6), ("back", 0, 1), ("front",), ("sum", 3, 0), ("sum", 4, 0), ("send_p",), ("sum", 3, 1), ("take_p",),
-    ("sum", 4, 1), ("sum", 3, 2), ("sum", 4, 2), ("sum", 3, 3), ("sum_p", 0), ("sum", 3, 4), ("sum", 4, 3),
-    ("sum_p", 1), ("seq", 0, 1), ("sum", 4, 4), ("sum_p", 2), ("seq", 1, 2), ("weights",), ("tiny", 0), ("sum_p", 3),
+    ("ins", 1, 6), ("back", 0, 1), ("sum", 3, 0), ("front",), ("sum", 4, 0), ("sum", 3, 1), ("send_p",), ("take_p",),
+    ("sum", 4, 1), ("sum", 3, 2), ("sum_p", 0), ("sum", 4, 2), ("sum", 3, 3), ("sum", 4, 3), ("sum_p", 1),
+    ("sum", 3, 4), ("sum", 4, 4), ("seq", 0, 1), ("sum_p", 2), ("seq", 1, 2), ("sum_p", 3), ("weights",), ("tiny", 0),
     ("sum_p", 4), ("tiny", 1), ("tiny", 2), ("all_p", 1), ("tiny", 3), ("all_p", 2), ("tiny", 4), ("all_p", 3),
     ("tiny", 5), ("all_p", 4), ("tiny", 6),
 )
 PLAN_SECOND = (
-    ("outs", 0, 6), ("send_t", 0), ("back", 0, 1), ("send_i", 0), ("sum", 0, 0), ("take_t", 0), ("take_i", 0),
-    ("sum", 1, 0), ("back", 3, 6), ("sum", 0, 1), ("back", 1, 3), ("sum", 1, 1), ("sum", 2, 0), ("sum", 0, 2),
-    ("front",), ("sum", 1, 2), ("send_v",), ("sum", 2, 1), ("sum", 0, 3), ("take_v",), ("sum", 1, 3), ("sum", 2, 2),
-    ("sum", 0, 4), ("sum_v", 0), ("sum", 1, 4), ("sum", 2, 3), ("sum_v", 1), ("all", 0, 1), ("all", 1, 1),
-    ("sum", 2, 4), ("sum_v", 2), ("all", 3, 0), ("all", 0, 2), ("all", 3, 1), ("sum_v", 3), ("all", 4, 0),
-    ("all", 2, 1), ("all", 1, 2), ("sum_v", 4), ("all", 4, 1), ("all", 2, 2), ("all_v", 1), ("all", 4, 2),
-    ("all_v", 2), ("all", 1, 3), ("all", 3, 2), ("all", 0, 3), ("all_v", 3), ("all", 4, 3), ("all_v", 4),
-    ("all", 2, 3), ("all", 1, 4), ("all", 3, 3), ("all", 0, 4), ("all", 2, 4), ("all", 4, 4), ("all", 3, 4),
+    ("send_t", 0), ("send_o", 0), ("send_o", 4), ("send_o", 1), ("take_t", 0), ("back", 0, 1), ("send_o", 2),
+    ("send_o", 3), ("take_o", 0), ("take_o", 4), ("take_o", 1), ("send_o", 5), ("send_i", 0), ("take_o", 2),
+    ("take_o", 3), ("back", 1, 3), ("take_i", 0), ("take_o", 5), ("back", 3, 6), ("sum", 0, 0), ("sum", 1, 0),
+    ("front",), ("sum", 2, 0), ("sum", 0, 1), ("sum", 1, 1), ("sum", 2, 1), ("sum", 0, 2), ("sum", 1, 2),
+    ("sum", 2, 2), ("sum", 0, 3), ("send_v",), ("sum", 1, 3), ("sum", 2, 3), ("take_v",), ("sum", 0, 4),
+    ("sum", 1, 4), ("sum", 2, 4), ("all", 0, 1), ("all", 1, 1), ("sum_v", 0), ("all", 3, 0), ("all", 2, 1),
+    ("all", 0, 2), ("all", 4, 0), ("all", 1, 2), ("all", 3, 1), ("sum_v", 1), ("sum_v", 2), ("all", 2, 2),
+    ("sum_v", 3), ("all", 4, 1), ("all", 1, 3), ("sum_v", 4), ("all", 0, 3), ("all", 3, 2), ("all", 4, 2),
+    ("all", 1, 4), ("all_v", 1), ("all", 3, 3), ("all", 2, 3), ("all_v", 2), ("all", 4, 3), ("all_v", 3),
+    ("all", 0, 4), ("all", 2, 4), ("all", 3, 4), ("all_v", 4), ("all", 4, 4),
 )
 
 
@@ -795,17 +797,9 @@
         def backs(start, end):
             lax.fori_loop(start, end, expert_backward, 0)
 
-        def outs(start, end):
-            @pl.loop(start, end + 1)
-            def _(e):
-                @pl.when(e < end)
-                def _():
-                    spread_residual(e, 0)
-                    big.send(e, 2 * e, out_halves(e, 1 - core))
-
-                @pl.when(e > start)
-                def _():
-                    big.take(e - 1, 2 * e - 2, out_halves(e - 1, core))
+        def send_out(e):
+            spread_residual(e, 0)
+            big.send(e, 2 * e, out_halves(e, 1 - core))
 
         def ins(start, end):
             @pl.loop(start, end + 1)
@@ -821,7 +815,8 @@
                     big.take(5 + e, IN_UNIT + 2 * e - 2, in_halves(e - 1, core))
 
         work = {
-            "outs": outs,
+            "send_o": send_out,
+            "take_o": lambda e: big.take(e, 2 * e, out_halves(e, core)),
             "ins": ins,
             "send_t": lambda e: big.send(12, TOWER_UNIT, tower_halves(1 - core)),
             "take_t": lambda e: big.take(12, TOWER_UNIT, tower_halves(core)),

time: 90.9 us -> 94.6 us (1.041)
  Pallas kernels: 89.9 us -> 93.2 us
    pallas_call x1, Pallas kernels: 79.2 us -> 82.5 us  [run(): pl.pallas_call(kernel, out_shape=outs, in_specs=[here] * 16 + [far] * 6,...]
where the time goes in v4:
time: 94.6 us; the launch traced here: 94.1 us
  Pallas kernels  93.2 us (99%)
    pallas_call x1, Pallas kernels, run(): pl.pallas_call(kernel, out_shape=outs, in_specs=[here] * 16 + [far] * 6,...  82.5 us
    pallas_call x1, Pallas kernels, place(): pl.pallas_call(place_kernel, out_shape=[jax.ShapeDtypeStruct(shape, F32)...  10.7 us

profile of v4, /device:TPU:65, one launch (start us, length us, event | category | flops | bytes accessed | tf_op | source)
XLA Modules:
  0.0 94.1 jit_solution(1448652867877423158)
XLA Ops:
  0.7 82.5 %rank_and_sum.1 = (bf16[25,2,1024,128]{3,2,1,0:T(8,128)(2,1)S(1)}, bf16[5,2,256,128]{3,2,1,0:T(8,128)(2,1)S(1)}, f32[1,2,128,128]{3,2,1,0:T(8,128)S(1)}, f32[24,...) custom-call(s32[1,256]{1,0:T(1,128)} %bitcast.20, ...), custom_call_target="tpu_custom_call" | custom-call | tf_op jit(solution)/shard_map/rank_and_sum/pallas_call | solution.py:936
  83.2 10.7 %place.1 = (f32[1,6,1024,512]{3,2,1,0:T(8,128)}, f32[1,6,512,1024]{3,2,1,0:T(8,128)}, f32[1,256,640]{2,1,0:T(8,128)}, f32[1,256,3200]{2,1,0:T(8,128)}, f32[1,640...) custom-call(bf16[25,2,1024,128]{3,2,1,0:T(8,128)(2,1)S(1)} %get-tupl, ...), custom_call_target="tpu_custom_call" | custom-call | tf_op jit(solution)/shard_map/place/pallas_call | solution.py:1134
